TPU v7x, 32 devices: a whole 2x2x4 slice. The times are simulated.
32 devices in a mesh: gx: 4 (over z), gy: 8 (over y, x, core).
Axes of the slice: x: 2, y: 2, z: 4, core: 2. Of those that a mesh axis runs over, the one named last changes fastest.
Arguments:
- multipoles: float32 [56, 40960], P(None, ('gx', 'gy')), may hold values from -6 to 6
- trans: float32 [316, 56, 56], replicated, may hold values from -0.078125 to 0.078125
- pair_target: int32 [316, 8192], P(None, ('gx', 'gy')), may hold values from -1 to 1279, as said below
- pair_source: int32 [316, 8192], P(None, ('gx', 'gy')), may hold values from -1 to 2815, as said below
- send_list: int32 [32, 1536], P(('gx', 'gy')), may hold values from 0 to 1279
Outputs:
- locals_out: float32 [56, 40960], P(None, ('gx', 'gy'))
Inputs may be any that keep to these rules, and one draw needn't show every extreme that they name: `pair_target`: in each offset, the used slots of a device come first; in every offset some device uses all 256 slots. Unused slots hold -1 in both lists. `pair_source`: -1 exactly where pair_target is -1. A position past 1280 lies among the first entries of its block, up to a live count of that block which differs from device to device and block to block (from zero to 128; zero for the block from the device itself and for neighbours past either end of gy; 128 for some block of every device).
All inputs are finite; a program needn't handle non-finite values.
Results may differ from a plain program's by a relative error of at most 0.0003.
Values sent between devices are 32-bit elements; how exact they have to be, the bound alone decides.
No kernel may reach another device: no remote copies, remote signals or barrier semaphores. Data moves between devices by JAX's collectives and lax.ppermute only.
A program may use at most 128 MiB of HBM per device.

v0:
```python
import jax
import jax.numpy as jnp
from jax import lax
from jax.sharding import PartitionSpec as P

REACH = 4


def parity_signs(term_count):
    term_index = jnp.arange(term_count, dtype=jnp.int32)
    degree = (term_index >= 1).astype(jnp.int32) + (term_index >= 4).astype(jnp.int32)
    degree = degree + (term_index >= 10).astype(jnp.int32) + (term_index >= 20).astype(jnp.int32)
    degree = degree + (term_index >= 35).astype(jnp.int32)
    return jnp.where(degree % 2 == 0, 1.0, -1.0).astype(jnp.float32)


def per_device(multipoles, trans, pair_target, pair_source, send_list):
    term_count, cell_count = multipoles.shape
    outer_count = lax.axis_size("gx")
    inner_count = lax.axis_size("gy")
    peer_count = outer_count * inner_count
    near_count = outer_count + 2 * REACH
    sent_rows = send_list[0]
    halo_width = sent_rows.shape[0] // near_count
    packed = jnp.take(multipoles, sent_rows, axis=1).reshape(term_count, near_count, halo_width)
    outer_here = lax.axis_index("gx")
    inner_here = lax.axis_index("gy")
    steps_up = jnp.arange(1, REACH + 1, dtype=jnp.int32)
    outer_ids = jnp.arange(outer_count, dtype=jnp.int32) * inner_count + inner_here
    self_id = outer_here * inner_count + inner_here
    send_ids = jnp.concatenate([outer_ids, self_id - steps_up, self_id + steps_up])
    send_valid = jnp.concatenate(
        [
            jnp.ones((outer_count,), bool),
            inner_here - steps_up >= 0,
            inner_here + steps_up < inner_count,
        ]
    )
    send_safe = jnp.where(send_valid, send_ids, peer_count)
    from_ids = jnp.concatenate([outer_ids, self_id + steps_up, self_id - steps_up])
    from_valid = jnp.concatenate(
        [
            jnp.ones((outer_count,), bool),
            inner_here + steps_up < inner_count,
            inner_here - steps_up >= 0,
        ]
    )
    from_safe = jnp.where(from_valid, from_ids, peer_count)
    from_mask = from_valid.astype(jnp.float32)[None, :, None]
    send_mask = send_valid.astype(jnp.float32)[None, :, None]
    spread = (
        jnp.zeros((term_count, peer_count, halo_width), jnp.float32)
        .at[:, send_safe]
        .set(packed, mode="drop")
    )
    landed = lax.all_to_all(spread, ("gx", "gy"), split_axis=1, concat_axis=1, tiled=True)
    arrived = jnp.take(landed, jnp.minimum(from_safe, peer_count - 1), axis=1) * from_mask
    buffer = jnp.concatenate(
        [multipoles, arrived.reshape(term_count, near_count * halo_width)], axis=1
    )
    parity = parity_signs(term_count)[:, None, None]
    offset_count = trans.shape[0]
    block_count = 4
    block_size = offset_count // block_count

    def one_block(totals, pieces):
        matrices, target, source = pieces
        usable = (target >= 0).astype(jnp.float32)[None]
        target_idx = jnp.maximum(target, 0)
        source_idx = jnp.maximum(source, 0)
        source_cols = jnp.take(buffer, source_idx, axis=1)
        target_cols = jnp.take(multipoles, target_idx, axis=1)
        forward = (
            jnp.einsum("oij,jos->ios", matrices, source_cols, precision=lax.Precision.HIGHEST)
            * usable
        )
        backward = (
            parity
            * jnp.einsum(
                "oij,jos->ios", matrices, parity * target_cols, precision=lax.Precision.HIGHEST
            )
            * usable
        )
        totals = totals.at[:, target_idx].add(forward)
        totals = totals.at[:, source_idx].add(backward)
        return (totals, None)

    start = jnp.zeros((term_count, cell_count + near_count * halo_width), jnp.float32)
    blocked = (
        trans.reshape(block_count, block_size, term_count, term_count),
        pair_target.reshape(block_count, block_size, -1),
        pair_source.reshape(block_count, block_size, -1),
    )
    totals, _ = lax.scan(one_block, start, blocked)
    outgoing = totals[:, cell_count:].reshape(term_count, near_count, halo_width)
    spread_back = (
        jnp.zeros((term_count, peer_count, halo_width), jnp.float32)
        .at[:, from_safe]
        .set(outgoing * from_mask, mode="drop")
    )
    landed_back = lax.all_to_all(spread_back, ("gx", "gy"), split_axis=1, concat_axis=1, tiled=True)
    returned = jnp.take(landed_back, jnp.minimum(send_safe, peer_count - 1), axis=1) * send_mask
    return (
        totals[:, :cell_count]
        .at[:, sent_rows]
        .add(returned.reshape(term_count, near_count * halo_width))
    )


def solution(mesh):
    placed = (
        P(None, ("gx", "gy")),
        P(),
        P(None, ("gx", "gy")),
        P(None, ("gx", "gy")),
        P(("gx", "gy"), None),
    )
    return jax.shard_map(
        per_device, mesh=mesh, in_specs=placed, out_specs=P(None, ("gx", "gy")), check_vma=False
    )
```

profile of v0, /device:TPU:0, one launch (start us, length us, event | category | flops | bytes accessed | tf_op | source)
XLA Modules:
  0.0 1749.5 jit_solution(1294562083332527434)
XLA Ops:
  16.9 12.0 copy.23
  41.6 1666.9 %while.12 = (s32[]{:T(128)}, f32[56,2816]{0,1:T(8,128)S(1)}, s32[4,79,256]{2,1,0:T(8,128)}, s32[4,79,256]{2,1,0:T(8,128)}, f32[56,2816]{0,1:T(8,128)S(1)}, /*ind...) while((s32[]{:T(128)}, f32[56,2816]{0,1:T(8,128)S(1)}, ...), condition=%wide.region_4.6_spmd.clone.clone, body=%wide.region_1.0_spmd.clone.clone.sunk | while | flops 1531363328 | bytes 105818936 | solution.py:94
  46.5 41.5 %gather_fusion = f32[20224,56]{1,0:T(8,128)} fusion(f32[56,2816]{0,1:T(8,128)S(1)} %get-tuple-element.218, s32[20480]{0:T(1024)} %pad_clamp_fusion.7), kind=kCustom, calls=%fused_computation.1.clone.clone.1 | custom fusion | bytes 9141248 | tf_op jit(solution)/shard_map/while/body/eval_jaxpr/jit(_take)/gather | solution.py:71
  96.8 9.6 broadcast_multiply_fusion.2
  116.0 135.9 %scatter_fusion = f32[56,2816]{0,1:T(8,128)S(1)} fusion(f32[56,2816]{0,1:T(8,128)S(1)} %get-tuple-element.207, s32[20224]{0:T(1024)} %reshape.498, f32[20224,56]{1,0:T(8,128)} %bitcast.110), kind=kCustom, calls=%fused_computation.5.clone.clone.1 | custom fusion | flops 1132544 | bytes 13671424 | tf_op jit(solution)/shard_map/while/body/eval_jaxpr/scatter-add | solution.py:84
  253.4 41.5 %gather_fusion.1 = f32[20224,56]{1,0:T(8,128)} fusion(f32[56,1280]{0,1:T(8,128)S(1)} %get-tuple-element.220, s32[20480]{0:T(1024)} %pad_clamp_fusion.8), kind=kCustom, calls=%fused_computation.2.clone.clone.1 | custom fusion | bytes 9141248 | tf_op jit(solution)/shard_map/while/body/eval_jaxpr/jit(_take)/gather | solution.py:72
  303.8 10.1 multiply_multiply_fusion.2
  321.9 135.9 %scatter_fusion.1 = f32[56,2816]{0,1:T(8,128)S(1)} fusion(f32[56,2816]{0,1:T(8,128)S(1)} %scatter_fusion, s32[20224]{0:T(1024)} %reshape.499, f32[20224,56]{1,0:T(8,128)} %bitcast.111), kind=kCustom, calls=%fused_computation.6.clone.clone.1 | custom fusion | flops 1132544 | bytes 13671424 | tf_op jit(solution)/shard_map/while/body/eval_jaxpr/scatter-add | solution.py:85
  462.5 41.5 %gather_fusion = f32[20224,56]{1,0:T(8,128)} fusion(f32[56,2816]{0,1:T(8,128)S(1)} %get-tuple-element.218, s32[20480]{0:T(1024)} %pad_clamp_fusion.7), kind=kCustom, calls=%fused_computation.1.clone.clone.1 | custom fusion | bytes 9141248 | tf_op jit(solution)/shard_map/while/body/eval_jaxpr/jit(_take)/gather | solution.py:71
  532.0 136.4 %scatter_fusion = f32[56,2816]{0,1:T(8,128)S(1)} fusion(f32[56,2816]{0,1:T(8,128)S(1)} %get-tuple-element.207, s32[20224]{0:T(1024)} %reshape.498, f32[20224,56]{1,0:T(8,128)} %bitcast.110), kind=kCustom, calls=%fused_computation.5.clone.clone.1 | custom fusion | flops 1132544 | bytes 13671424 | tf_op jit(solution)/shard_map/while/body/eval_jaxpr/scatter-add | solution.py:84
  670.0 41.5 %gather_fusion.1 = f32[20224,56]{1,0:T(8,128)} fusion(f32[56,1280]{0,1:T(8,128)S(1)} %get-tuple-element.220, s32[20480]{0:T(1024)} %pad_clamp_fusion.8), kind=kCustom, calls=%fused_computation.2.clone.clone.1 | custom fusion | bytes 9141248 | tf_op jit(solution)/shard_map/while/body/eval_jaxpr/jit(_take)/gather | solution.py:72
  720.3 10.1 multiply_multiply_fusion.2
  738.4 136.4 %scatter_fusion.1 = f32[56,2816]{0,1:T(8,128)S(1)} fusion(f32[56,2816]{0,1:T(8,128)S(1)} %scatter_fusion, s32[20224]{0:T(1024)} %reshape.499, f32[20224,56]{1,0:T(8,128)} %bitcast.111), kind=kCustom, calls=%fused_computation.6.clone.clone.1 | custom fusion | flops 1132544 | bytes 13671424 | tf_op jit(solution)/shard_map/while/body/eval_jaxpr/scatter-add | solution.py:85
  879.6 41.5 %gather_fusion = f32[20224,56]{1,0:T(8,128)} fusion(f32[56,2816]{0,1:T(8,128)S(1)} %get-tuple-element.218, s32[20480]{0:T(1024)} %pad_clamp_fusion.7), kind=kCustom, calls=%fused_computation.1.clone.clone.1 | custom fusion | bytes 9141248 | tf_op jit(solution)/shard_map/while/body/eval_jaxpr/jit(_take)/gather | solution.py:71
  949.1 135.9 %scatter_fusion = f32[56,2816]{0,1:T(8,128)S(1)} fusion(f32[56,2816]{0,1:T(8,128)S(1)} %get-tuple-element.207, s32[20224]{0:T(1024)} %reshape.498, f32[20224,56]{1,0:T(8,128)} %bitcast.110), kind=kCustom, calls=%fused_computation.5.clone.clone.1 | custom fusion | flops 1132544 | bytes 13671424 | tf_op jit(solution)/shard_map/while/body/eval_jaxpr/scatter-add | solution.py:84
  1086.5 41.5 %gather_fusion.1 = f32[20224,56]{1,0:T(8,128)} fusion(f32[56,1280]{0,1:T(8,128)S(1)} %get-tuple-element.220, s32[20480]{0:T(1024)} %pad_clamp_fusion.8), kind=kCustom, calls=%fused_computation.2.clone.clone.1 | custom fusion | bytes 9141248 | tf_op jit(solution)/shard_map/while/body/eval_jaxpr/jit(_take)/gather | solution.py:72
  1136.8 10.1 multiply_multiply_fusion.2
  1154.9 135.9 %scatter_fusion.1 = f32[56,2816]{0,1:T(8,128)S(1)} fusion(f32[56,2816]{0,1:T(8,128)S(1)} %scatter_fusion, s32[20224]{0:T(1024)} %reshape.499, f32[20224,56]{1,0:T(8,128)} %bitcast.111), kind=kCustom, calls=%fused_computation.6.clone.clone.1 | custom fusion | flops 1132544 | bytes 13671424 | tf_op jit(solution)/shard_map/while/body/eval_jaxpr/scatter-add | solution.py:85
  1295.5 41.5 %gather_fusion = f32[20224,56]{1,0:T(8,128)} fusion(f32[56,2816]{0,1:T(8,128)S(1)} %get-tuple-element.218, s32[20480]{0:T(1024)} %pad_clamp_fusion.7), kind=kCustom, calls=%fused_computation.1.clone.clone.1 | custom fusion | bytes 9141248 | tf_op jit(solution)/shard_map/while/body/eval_jaxpr/jit(_take)/gather | solution.py:71
  1365.0 136.6 %scatter_fusion = f32[56,2816]{0,1:T(8,128)S(1)} fusion(f32[56,2816]{0,1:T(8,128)S(1)} %get-tuple-element.207, s32[20224]{0:T(1024)} %reshape.498, f32[20224,56]{1,0:T(8,128)} %bitcast.110), kind=kCustom, calls=%fused_computation.5.clone.clone.1 | custom fusion | flops 1132544 | bytes 13671424 | tf_op jit(solution)/shard_map/while/body/eval_jaxpr/scatter-add | solution.py:84
  1503.2 41.5 %gather_fusion.1 = f32[20224,56]{1,0:T(8,128)} fusion(f32[56,1280]{0,1:T(8,128)S(1)} %get-tuple-element.220, s32[20480]{0:T(1024)} %pad_clamp_fusion.8), kind=kCustom, calls=%fused_computation.2.clone.clone.1 | custom fusion | bytes 9141248 | tf_op jit(solution)/shard_map/while/body/eval_jaxpr/jit(_take)/gather | solution.py:72
  1553.5 10.1 multiply_multiply_fusion.2
  1571.6 136.6 %scatter_fusion.1 = f32[56,2816]{0,1:T(8,128)S(1)} fusion(f32[56,2816]{0,1:T(8,128)S(1)} %scatter_fusion, s32[20224]{0:T(1024)} %reshape.499, f32[20224,56]{1,0:T(8,128)} %bitcast.111), kind=kCustom, calls=%fused_computation.6.clone.clone.1 | custom fusion | flops 1132544 | bytes 13671424 | tf_op jit(solution)/shard_map/while/body/eval_jaxpr/scatter-add | solution.py:85
  1715.2 23.4 %all-to-all-done.1 = f32[56,32,128]{2,0,1:T(8,128)S(1)} async-done(((f32[56,32,128]{2,0,1:T(8,128)}), f32[56,32,128]{2,0,1:T(8,128)S(1)}, u32[]{:S(2)}, u32[]{:S(2)}) %all-to-all-start.1) | async-done | bytes 917536 | tf_op jit(solution)/shard_map/all_to_all | solution.py:101
  (113 shorter events, 241.6 us)
Async XLA Ops:
  0.0 5.4 copy-start.7
  1.2 8.4 copy-start
  2.0 0.6 copy-start.5
  9.7 30.6 %all-to-all-start = ((f32[56,32,128]{2,0,1:T(8,128)}), f32[56,32,128]{2,0,1:T(8,128)S(1)}, u32[]{:S(2)}, u32[]{:S(2)}) async-start(f32[56,32,128]{2,0,1:T(8,128)} %scatter_fusion.2), calls=%async_computation | async-start | bytes 1835008 | tf_op jit(solution)/shard_map/all_to_all | solution.py:56
  16.8 12.1 copy-start.3
  16.9 12.8 copy-start.4
  16.9 24.1 %copy-start.2 = (f32[56,1280]{1,0:T(8,128)S(1)}, f32[56,1280]{1,0:T(8,128)}, u32[]{:S(2)}) copy-start(f32[56,1280]{1,0:T(8,128)} %param.9) | copy-start | bytes 860164
  28.9 12.7 copy-start.1
  31.1 9.8 copy-start.8
  41.6 1667.2 %copy-start.9 = (f32[12]{0:T(128)S(1)}, f32[12]{0:T(128)}, u32[]{:S(2)}) copy-start(f32[12]{0:T(128)} %copy-done.8) | copy-start | bytes 148
  41.6 1668.3 %copy-start.10 = (s32[12]{0:T(128)S(1)}, s32[12]{0:T(128)}, u32[]{:S(2)}) copy-start(s32[12]{0:T(128)} %get-tuple-element.129) | copy-start | bytes 148
  1708.5 6.7 copy-start.11
  1708.5 30.7 %copy-start.12 = (f32[12]{0:T(128)S(1)}, f32[12]{0:T(128)}, u32[]{:S(2)}) copy-start(f32[12]{0:T(128)} %get-tuple-element.131) | copy-start | bytes 148
  1708.5 30.7 %copy-start.13 = (pred[12]{0:T(512)(128)(4,1)S(1)}, pred[12]{0:T(512)(128)(4,1)}, u32[]{:S(2)}) copy-start(pred[12]{0:T(512)(128)(4,1)} %get-tuple-element.135) | copy-start | bytes 40
  1708.8 30.7 %copy-start.6 = (s32[1536]{0:T(1024)S(1)}, s32[1536]{0:T(1024)}, u32[]{:S(2)}) copy-start(s32[1536]{0:T(1024)} %copy-done.5) | copy-start | bytes 18436
  1712.4 26.1 %all-to-all-start.1 = ((f32[56,32,128]{2,0,1:T(8,128)}), f32[56,32,128]{2,0,1:T(8,128)S(1)}, u32[]{:S(2)}, u32[]{:S(2)}) async-start(f32[56,32,128]{2,0,1:T(8,128)} %scatter_fusion.3), calls=%async_computation.1 | async-start | bytes 1835008 | tf_op jit(solution)/shard_map/all_to_all | solution.py:101
where the time goes:
time: 1760 us; the launch traced here: 1750 us
  other arithmetic  1120 us (64%)
  local copies, waits for them, and re-layouts  507 us (29%)
  matrix products  78.7 us (4%)
  waiting for transfers between devices  32.5 us (2%)
    scatter-add x4, other arithmetic, one_block(): totals = totals.at[:, source_idx].add(backward)  545 us
    scatter-add x4, other arithmetic, one_block(): totals = totals.at[:, target_idx].add(forward)  545 us
    gather x8, local copies, waits for them, and re-layouts, one_block(): source_cols = jnp.take(buffer, source_idx, axis=1)  201 us
    gather x8, local copies, waits for them, and re-layouts, one_block(): target_cols = jnp.take(multipoles, target_idx, axis=1)  201 us
    dot_general x4, matrix products, one_block(): jnp.einsum('oij,jos->ios', matrices, parity * target_cols, precision=lax....  40.2 us
    dot_general x4, matrix products, one_block(): jnp.einsum('oij,jos->ios', matrices, source_cols, precision=lax.Precision...  38.5 us
  transfers between devices with their start and end apart: 2, of which 2 were waited for; matrix products, arithmetic and copies ran while one was open for 1% of the time, Pallas kernels for 0%

commit v1 on v0

v1 whole, which is shorter than its diff:
```python
import functools

import jax
import jax.numpy as jnp
from jax import lax
from jax.experimental import pallas as pl
from jax.experimental.pallas import tpu as pltpu
from jax.sharding import PartitionSpec as P

REACH = 4
LANES = 128
SUBLANES = 16
WIDTH = 1024
GRAIN = 32
FOLD = 256
SCRATCHES = 14
SHORT = 64
PACK_LIMIT = 60 * 1024 * 1024
VMEM_LIMIT = 53 * 1024 * 1024
SMALL_LIMIT = 16 * 1024 * 1024


def parity_signs(term_count):
    term_index = jnp.arange(term_count, dtype=jnp.int32)
    degree = (term_index >= 1).astype(jnp.int32) + (term_index >= 4).astype(jnp.int32)
    degree = degree + (term_index >= 10).astype(jnp.int32) + (term_index >= 20).astype(jnp.int32)
    degree = degree + (term_index >= 35).astype(jnp.int32)
    return jnp.where(degree % 2 == 0, 1.0, -1.0).astype(jnp.float32)


def hot_columns(places, size):
    count = places[0].shape[1]
    tall = (SUBLANES, count)
    one, none = jnp.ones((), jnp.bfloat16), jnp.zeros((), jnp.bfloat16)
    row = lax.broadcasted_iota(jnp.int32, tall, 0).astype(jnp.float32)
    rows = [(row + float(k)).astype(jnp.bfloat16) for k in range(0, size, SUBLANES)]
    blocks = []
    for place in places:
        wanted = jnp.broadcast_to(place.astype(jnp.float32), tall).astype(jnp.bfloat16)
        blocks += [jnp.where(one_row == wanted, one, none) for one_row in rows]
    return jnp.concatenate(blocks, axis=0)


def stack_parts(values):
    high = values.astype(jnp.bfloat16).astype(jnp.float32)
    return jnp.concatenate([high, values - high], axis=0).astype(jnp.bfloat16)


def scatter_product(index_row, half, parts):
    rows, count = parts.shape
    upper = jnp.broadcast_to(index_row >= half, (rows, count))
    none = jnp.zeros((), jnp.bfloat16)
    pad = jnp.zeros((LANES - rows, count), jnp.bfloat16)
    spread = jnp.concatenate([jnp.where(upper, none, parts), pad, jnp.where(upper, parts, none), pad], axis=0)
    place = jnp.where(index_row >= half, index_row - half, index_row)
    hot = hot_columns([place - j * LANES for j in range(half // LANES)], LANES)
    return lax.dot_general(
        hot, spread, (((1,), (1,)), ((), ())), preferred_element_type=jnp.float32
    )


def unfold(acc_ref, terms):
    sides = []
    for side in range(2):
        turned = acc_ref[:, side * LANES : (side + 1) * LANES].T
        sides.append(turned[:terms] + turned[terms : 2 * terms])
    return jnp.concatenate(sides, axis=1)


def pick(options, which):
    chosen = options[0]
    for k in range(1, len(options)):
        chosen = jnp.where(which == k, options[k], chosen)
    return chosen


def batch_of(count, most):
    return max(k for k in range(1, most + 1) if count % k == 0)


def compact(starts_ref, tables):
    offset_count, slot_count = tables[0][0].shape
    pieces = slot_count // LANES
    for _, out_ref in tables:
        out_ref[...] = jnp.full(out_ref.shape, -1, jnp.int32)
    lane = lax.broadcasted_iota(jnp.int32, (8, LANES), 1)
    empty = jnp.full((8, LANES), -1, jnp.int32)
    batch = batch_of(offset_count, 4)

    def place(step, kept):
        kept = list(kept)
        for u in range(batch):
            offset = step * batch + u
            start = starts_ref[offset]
            row, shift = start >> 7, start & (LANES - 1)
            crossed = (starts_ref[offset + 1] >> 7) - row
            inside = lane >= shift
            for k, (pairs_ref, out_ref) in enumerate(tables):
                line = pairs_ref[pl.ds(offset, 1), :]
                turned = [
                    pltpu.roll(jnp.broadcast_to(line[:, q * LANES : (q + 1) * LANES], (8, LANES)), shift, 1)
                    for q in range(pieces)
                ]
                turned = [kept[k], *turned, empty]
                tiles = [jnp.where(inside, turned[q + 1], turned[q]) for q in range(pieces + 1)]
                for q, tile in enumerate(tiles):
                    out_ref[pl.ds(row + q, 1), :] = tile[:1]
                kept[k] = pick(tiles, crossed)
        return tuple(kept)

    lax.fori_loop(0, offset_count // batch, place, (empty,) * len(tables))


def turn_matrices(t_ref, matrix_ref):
    terms, _, offset_count = t_ref.shape
    turns = batch_of(terms, 4)
    pad = jnp.zeros((LANES - 2 * terms, offset_count), jnp.float32)

    def turn(step, carry):
        for u in range(turns):
            i = step * turns + u
            block = t_ref[i]
            matrix_ref[pl.ds(i, offset_count, stride=terms), :] = jnp.concatenate([block, block, pad], axis=0).T
        return carry

    lax.fori_loop(0, terms // turns, turn, 0)


def index_row(ref, first, count):
    return jnp.concatenate([ref[pl.ds(first + q, 1), :] for q in range(count)], axis=1)


def gather_columns(parts, index):
    terms = parts[0].shape[0]
    lane = jnp.broadcast_to(index & (LANES - 1), (terms, LANES))
    chunk = jnp.broadcast_to(index >> 7, (8, LANES))
    picked = [jnp.zeros((8, LANES), jnp.float32)] * (terms // 8)
    for c, part in enumerate(parts):
        found = jnp.take_along_axis(part[...], lane, axis=1, mode="promise_in_bounds")
        here = chunk == c
        picked = [jnp.where(here, found[8 * r : 8 * r + 8], some) for r, some in enumerate(picked)]
    return jnp.concatenate(picked, axis=0)


def fold_columns(fold_ref, parts, index):
    count = index.shape[1]
    hot = hot_columns([index & (FOLD - 1)], FOLD)
    found = jnp.dot(fold_ref[...], hot, preferred_element_type=jnp.float32)
    chunk = jnp.broadcast_to(index >> (FOLD.bit_length() - 1), (8, count))
    masks = [chunk == c for c in range(fold_ref.shape[0] // parts)]
    picked = []
    for r in range(0, parts, 8):
        some = jnp.zeros((8, count), jnp.float32)
        for c, mask in enumerate(masks):
            some = jnp.where(mask, found[c * parts + r : c * parts + r + 8], some)
        picked.append(some)
    return jnp.concatenate(picked, axis=0).astype(jnp.bfloat16)


def block_for(place, here, sign):
    distance = (place - here) * sign
    block = jnp.where(distance > 0, distance - 1, REACH - 1 - distance)
    there = (distance != 0) & (distance <= REACH) & (distance >= -REACH)
    return jnp.where(there, block, 0), there


def sender_of(block, here, sign, count):
    step = block + 1 if block < REACH else REACH - 1 - block
    place = here - step * sign
    return jnp.clip(place, 0, count - 1), (place >= 0) & (place < count)


def turned(place, count):
    return jnp.where(place >= count, place - count, jnp.where(place < 0, place + count, place))


def upper_blocks(here, count):
    return jnp.minimum(count - 1 - here, REACH)


def rank_of(block, here_ref, outer_count, inner_count):
    outer = block - jnp.where(block > here_ref[0], 1, 0)
    lower = block - 1 - REACH + upper_blocks(here_ref[1], inner_count)
    return jnp.where(block < outer_count, outer, jnp.where(block < outer_count + REACH, block - 1, lower))


def most_blocks(outer_count, inner_count):
    along = [min(REACH, inner_count - 1 - p) + min(REACH, p) for p in range(inner_count)]
    return outer_count - 1 + max(along)


def hand_out(read, here_ref, sign, outer_refs, inner_ref):
    outer_count = len(outer_refs) + 1
    for k, ref in enumerate(outer_refs):
        ref[...] = read(turned(here_ref[0] + k + 1, outer_count), True)

    def hand(place, carry):
        block, there = block_for(place, here_ref[1], sign)
        inner_ref[place] = read(outer_count + block, there)
        return carry

    lax.fori_loop(0, inner_ref.shape[0], hand, 0)


def take_in(put, here_ref, sign, outer_refs, inner_ref):
    outer_count = len(outer_refs) + 1
    for k, ref in enumerate(outer_refs):
        put(turned(here_ref[0] - k - 1, outer_count), True, ref[...])
    for block in range(2 * REACH):
        sender, there = sender_of(block, here_ref[1], sign, inner_ref.shape[0])
        put(outer_count + block, there, inner_ref[sender])


def translate_kernel(*refs):
    outer_count = (len(refs) - SCRATCHES - 11) // 2
    inputs, refs = refs[:9], refs[9:]
    outer_refs, refs = refs[:outer_count], refs[outer_count:]
    own_ref, inner_back_ref, refs = refs[0], refs[1], refs[2:]
    outer_back_refs, refs = refs[:outer_count], refs[outer_count:]
    translate_body(*inputs, outer_refs, own_ref, inner_back_ref, outer_back_refs, *refs)


def translate_body(
    starts_ref, offsets_ref, here_ref, pair_target_ref, pair_source_ref, trans_ref, multipoles_ref, sign_ref, inner_ref,
    outer_refs, own_ref, inner_back_ref, outer_back_refs,
    target_pairs_ref, source_pairs_ref, native_ref, x_ref, target_ref, source_ref, t_ref,
    fold_ref, near_ref, forward_ref, backward_ref, own_acc_ref, all_acc_ref, ready
):
    fetches = [
        pltpu.make_async_copy(here, there, ready.at[k])
        for k, (here, there) in enumerate(
            [
                (pair_target_ref, target_pairs_ref),
                (pair_source_ref, source_pairs_ref),
                (multipoles_ref, x_ref),
                (trans_ref, native_ref),
            ]
        )
    ]
    for fetch in fetches:
        fetch.start()
    terms, cells = x_ref.shape
    outer_count, inner_count = len(outer_refs) + 1, inner_ref.shape[0]
    spare = near_ref.shape[0] - 1
    chunks = cells // LANES
    own_half = cells // 2
    all_half = all_acc_ref.shape[0]
    parts = 2 * terms
    per_step = WIDTH // LANES
    grains = LANES // GRAIN

    for fetch in fetches[:3]:
        fetch.wait()
    folds = cells // FOLD
    for c in range(folds):
        fold_ref[c * parts : (c + 1) * parts, :] = stack_parts(x_ref[:, c * FOLD : (c + 1) * FOLD] * sign_ref[...])
    near_ref[...] = jnp.zeros_like(near_ref)

    def put(block, there, value):
        near_ref[jnp.where(there, rank_of(block, here_ref, outer_count, inner_count), spare)] = value

    take_in(put, here_ref, -1, outer_refs, inner_ref)
    own_acc_ref[...] = jnp.zeros_like(own_acc_ref)
    all_acc_ref[...] = jnp.zeros_like(all_acc_ref)
    forward_ref[...] = jnp.zeros_like(forward_ref)
    backward_ref[...] = jnp.zeros_like(backward_ref)

    def own_columns(ref):
        return [ref.at[:, c * LANES : (c + 1) * LANES] for c in range(chunks)]

    compact(starts_ref, [(target_pairs_ref, target_ref), (source_pairs_ref, source_ref)])
    position = source_ref[...]
    absent = REACH - upper_blocks(here_ref[1], inner_count)
    after_self = position >= cells + (here_ref[0] + 1) * LANES
    after_upper = position >= cells + (outer_count + REACH) * LANES
    source_ref[...] = position - jnp.where(after_self, LANES, 0) - jnp.where(after_upper, absent * LANES, 0)
    fetches[3].wait()
    turn_matrices(native_ref, t_ref)
    steps = (starts_ref[starts_ref.shape[0] - 1] + (WIDTH - 1)) // WIDTH
    low_lanes = lax.broadcasted_iota(jnp.int32, (terms, 2 * LANES), 1) & (LANES - 1)

    once = lax.broadcasted_iota(jnp.int32, (grains * terms, LANES), 1) < terms

    def scatter(group):
        first = jnp.maximum(group, 0) * per_step
        own_acc_ref[...] += scatter_product(index_row(target_ref, first, per_step), own_half, forward_ref[...])
        all_acc_ref[...] += scatter_product(index_row(source_ref, first, per_step), all_half, backward_ref[...])

    def step(group, carry):
        scatter(group - 1)
        ahead, back = [], []
        targets = fold_columns(fold_ref, parts, index_row(target_ref, group * per_step, per_step))
        for q in range(per_step):
            row = group * per_step + q
            sources = gather_columns(
                own_columns(x_ref) + [near_ref.at[k] for k in range(spare)], source_ref[pl.ds(row, 1), :]
            )
            columns = jnp.concatenate([stack_parts(sources), targets[:, q * LANES : (q + 1) * LANES]], axis=1)
            gap = jnp.zeros((LANES - parts, 2 * LANES), jnp.bfloat16)
            columns = jnp.concatenate([columns, gap, columns[:SHORT]], axis=0)
            high, low = [], []
            for g in range(grains):
                offset = offsets_ref[row * grains + g]
                matrix = t_ref[pl.ds(pl.multiple_of(offset * terms, 8), terms), :]
                high.append(matrix.astype(jnp.bfloat16).astype(jnp.float32))
                low.append(matrix - high[-1])
            high = jnp.concatenate(high, axis=0).astype(jnp.bfloat16)
            low = jnp.where(once, jnp.concatenate(low, axis=0), 0.0).astype(jnp.bfloat16)
            matrices = jnp.concatenate([high, low], axis=1)[:, : LANES + SHORT]
            moved = jnp.dot(matrices, columns, preferred_element_type=jnp.float32)
            total = moved[:terms]
            for g in range(1, grains):
                total = jnp.where(low_lanes >= g * GRAIN, moved[g * terms : (g + 1) * terms], total)
            total = stack_parts(total)
            ahead.append(total[:, :LANES])
            back.append(total[:, LANES:])
        for q in range(per_step):
            forward_ref[:, q * LANES : (q + 1) * LANES] = ahead[q]
            backward_ref[:, q * LANES : (q + 1) * LANES] = back[q]
        return carry

    lax.fori_loop(0, steps, step, 0)
    scatter(steps - 1)
    everywhere = unfold(all_acc_ref, terms) * sign_ref[...]
    own_ref[...] = unfold(own_acc_ref, terms) + everywhere[:, :cells]
    for k in range(spare):
        near_ref[k] = everywhere[:, cells + k * LANES : cells + (k + 1) * LANES]
    near_ref[spare] = jnp.zeros((terms, LANES), jnp.float32)

    def read(block, there):
        return near_ref[jnp.where(there, rank_of(block, here_ref, outer_count, inner_count), spare)]

    hand_out(read, here_ref, 1, outer_back_refs, inner_back_ref)


def translate(starts, offsets, here, pair_target, pair_source, trans, x, sign, inner, outer):
    terms, cells = x.shape
    offset_count = pair_target.shape[0]
    row_count = offsets.shape[0] * GRAIN // LANES
    hbm = pl.BlockSpec(memory_space=pltpu.HBM)
    outer_count = len(outer)
    near_count = most_blocks(outer_count + 1, inner.shape[0])
    own_half = cells // 2
    all_half = -(-(cells + near_count * LANES) // (2 * LANES)) * LANES
    smem = pl.BlockSpec(memory_space=pltpu.SMEM)
    vmem = pl.BlockSpec(memory_space=pltpu.VMEM)
    own, inner_back, *outer_back = pl.pallas_call(
        translate_kernel,
        out_shape=[jax.ShapeDtypeStruct(like.shape, jnp.float32) for like in (x, inner, *outer)],
        in_specs=[smem] * 3 + [hbm] * 4 + [vmem] * (2 + outer_count),
        out_specs=[vmem] * (2 + outer_count),
        scratch_shapes=[
            pltpu.VMEM(pair_target.shape, jnp.int32),
            pltpu.VMEM(pair_source.shape, jnp.int32),
            pltpu.VMEM((terms, terms, offset_count), jnp.float32),
            pltpu.VMEM((terms, cells), jnp.float32),
            pltpu.VMEM((row_count, LANES), jnp.int32),
            pltpu.VMEM((row_count, LANES), jnp.int32),
            pltpu.VMEM((offset_count * terms, LANES), jnp.float32),
            pltpu.VMEM((2 * terms * (cells // FOLD), FOLD), jnp.bfloat16),
            pltpu.VMEM((near_count + 1, terms, LANES), jnp.float32),
            pltpu.VMEM((2 * terms, WIDTH), jnp.bfloat16),
            pltpu.VMEM((2 * terms, WIDTH), jnp.bfloat16),
            pltpu.VMEM((own_half, 2 * LANES), jnp.float32),
            pltpu.VMEM((all_half, 2 * LANES), jnp.float32),
            pltpu.SemaphoreType.DMA((4,)),
        ],
        compiler_params=pltpu.CompilerParams(vmem_limit_bytes=VMEM_LIMIT),
        cost_estimate=pl.CostEstimate(flops=100_000_000_000, bytes_accessed=12_000_000, transcendentals=0),
    )(starts, offsets, here, pair_target, pair_source, trans.transpose(1, 2, 0), x, sign, inner, *outer)
    return own, inner_back, outer_back


def pack_kernel(here_ref, send_ref, multipoles_ref, inner_ref, *refs):
    outer_refs, (index_ref, x_ref, ready) = refs[:-3], refs[-3:]
    cells = x_ref.shape[1]
    fetches = [
        pltpu.make_async_copy(send_ref, index_ref, ready.at[0]),
        pltpu.make_async_copy(multipoles_ref, x_ref, ready.at[1]),
    ]
    for fetch in fetches:
        fetch.start()
    for fetch in fetches:
        fetch.wait()

    def read(block, there):
        index = index_ref[:, pl.ds(pl.multiple_of(block * LANES, LANES), LANES)]
        index = index if there is True else jnp.where(there, index, -1)
        return gather_columns([x_ref.at[:, c * LANES : (c + 1) * LANES] for c in range(cells // LANES)], index)

    hand_out(read, here_ref, -1, outer_refs, inner_ref)


def pack(here, index, x, outer_count, inner_count):
    smem = pl.BlockSpec(memory_space=pltpu.SMEM)
    vmem = pl.BlockSpec(memory_space=pltpu.VMEM)
    hbm = pl.BlockSpec(memory_space=pltpu.HBM)
    block = (x.shape[0], LANES)
    inner, *outer = pl.pallas_call(
        pack_kernel,
        out_shape=[jax.ShapeDtypeStruct((inner_count, *block), jnp.float32)]
        + [jax.ShapeDtypeStruct(block, jnp.float32)] * (outer_count - 1),
        in_specs=[smem, hbm, hbm],
        out_specs=[vmem] * outer_count,
        scratch_shapes=[
            pltpu.VMEM(index.shape, jnp.int32),
            pltpu.VMEM(x.shape, jnp.float32),
            pltpu.SemaphoreType.DMA((2,)),
        ],
        compiler_params=pltpu.CompilerParams(vmem_limit_bytes=PACK_LIMIT),
    )(here, index, x)
    return inner, outer


def collect_kernel(here_ref, index_ref, base_ref, inner_ref, *refs):
    outer_refs, (out_ref, near_ref, acc_ref) = refs[:-3], refs[-3:]
    terms, cells = base_ref.shape
    half = cells // 2
    near_ref[here_ref[0]] = jnp.zeros((terms, LANES), jnp.float32)

    def put(block, there, value):
        near_ref[block] = jnp.where(there, value, 0.0)

    take_in(put, here_ref, 1, outer_refs, inner_ref)
    parts = stack_parts(jnp.concatenate([near_ref[k] for k in range(near_ref.shape[0])], axis=1))
    acc_ref[...] = scatter_product(index_ref[...], half, parts)
    out_ref[...] = base_ref[...] + unfold(acc_ref, terms)


def collect(here, index, base, inner, outer):
    terms, cells = base.shape
    smem = pl.BlockSpec(memory_space=pltpu.SMEM)
    vmem = pl.BlockSpec(memory_space=pltpu.VMEM)
    return pl.pallas_call(
        collect_kernel,
        out_shape=jax.ShapeDtypeStruct(base.shape, jnp.float32),
        in_specs=[smem] + [vmem] * (3 + len(outer)),
        out_specs=vmem,
        scratch_shapes=[
            pltpu.VMEM((len(outer) + 1 + 2 * REACH, terms, LANES), jnp.float32),
            pltpu.VMEM((cells // 2, 2 * LANES), jnp.float32),
        ],
        compiler_params=pltpu.CompilerParams(vmem_limit_bytes=SMALL_LIMIT),
    )(here, index, base, inner, *outer)


def exchange(inner, outer):
    count = len(outer) + 1
    outer = [
        lax.ppermute(block, "gx", [(p, (p + k + 1) % count) for p in range(count)]) for k, block in enumerate(outer)
    ]
    return lax.all_to_all(inner, "gy", split_axis=0, concat_axis=0, tiled=True), outer


def per_device(multipoles, trans, pair_target, pair_source, send_list):
    offset_count, term_count, _ = trans.shape
    outer_count = lax.axis_size("gx")
    inner_count = lax.axis_size("gy")
    here = jnp.stack([lax.axis_index("gx"), lax.axis_index("gy")]).astype(jnp.int32)
    inner, outer = exchange(*pack(here, send_list, multipoles, outer_count, inner_count))

    used = jnp.sum((pair_target >= 0).astype(jnp.int32), axis=1)
    grains = (used + (GRAIN - 1)) // GRAIN
    ends = jnp.cumsum(grains)
    starts = jnp.concatenate([jnp.zeros((1,), jnp.int32), ends]) * GRAIN
    grain_count = -(-pair_target.size // WIDTH) * (WIDTH // GRAIN) + 2 * WIDTH // GRAIN
    grain_index = jnp.arange(grain_count, dtype=jnp.int32)
    offsets = jnp.sum((ends[None, :] <= grain_index[:, None]).astype(jnp.int32), axis=1)
    offsets = jnp.minimum(offsets, offset_count - 1)

    sign = parity_signs(term_count)[:, None]
    own, inner_back, outer_back = translate(
        starts, offsets, here, pair_target, pair_source, trans, multipoles, sign, inner, outer
    )
    return collect(here, send_list, own, *exchange(inner_back, outer_back))


def solution(mesh):
    placed = (
        P(None, ("gx", "gy")),
        P(),
        P(None, ("gx", "gy")),
        P(None, ("gx", "gy")),
        P(("gx", "gy"), None),
    )
    return jax.shard_map(
        per_device, mesh=mesh, in_specs=placed, out_specs=P(None, ("gx", "gy")), check_vma=False
    )
```

time: 1760 us -> 136 us (0.08)
  other arithmetic: 1120 us -> 2.74 us
  local copies, waits for them, and re-layouts: 507 us -> 0.89 us
  matrix products: 78.7 us -> 0 us
  Pallas kernels: 0 us -> 69 us
  starting transfers between devices: 9.87 us -> 59.5 us
  waiting for transfers between devices: 32.5 us -> 1.99 us
    scatter-add x9 -> x0, other arithmetic: 1100 us -> none  [the longest x4 545 us: one_block(): totals = totals.at[:, source_idx].add(backward)]
    gather x20 -> x0, local copies, waits for them, and re-layouts: 406 us -> none  [the longest x8 201 us: one_block(): source_cols = jnp.take(buffer, source_idx, axis=1)]
    dot_general x8 -> x0, matrix products: 78.7 us -> none  [the longest x4 40.2 us: one_block(): jnp.einsum('oij,jos->ios', matrices, parity * target_cols, precision=lax....]
    pallas_call x0 -> x3, Pallas kernels: none -> 69 us  [the longest x1 63 us: translate(): pl.pallas_call(translate_kernel, out_shape=[jax.ShapeDtypeStruct(like.sha...]
    mul x8 -> x0, local copies, waits for them, and re-layouts: 64.3 us -> none  [the longest x4 32.2 us: one_block(): jnp.einsum('oij,jos->ios', matrices, source_cols, precision=lax.Precision...]
    all_to_all x2, starting transfers between devices: 9.87 us -> 47.6 us  [exchange(): lax.all_to_all(inner, 'gy', split_axis=0, concat_axis=0, tiled=True)]
    all_to_all x2, waiting for transfers between devices: 32.5 us -> 0.01 us  [exchange(): lax.all_to_all(inner, 'gy', split_axis=0, concat_axis=0, tiled=True)]
  transfers between devices with their start and end apart: 2 -> 8, of which waited for: 2 -> 2; matrix products, arithmetic and copies ran while one was open for 1% -> 2% of each run, Pallas kernels for 0% -> 0%
where the time goes in v1:
time: 136 us; the launch traced here: 134 us
  Pallas kernels  69 us (51%)
  starting transfers between devices  59.5 us (44%)
  other arithmetic  2.74 us (2%)
  waiting for transfers between devices  1.99 us (1%)
    pallas_call x1, Pallas kernels, translate(): pl.pallas_call(translate_kernel, out_shape=[jax.ShapeDtypeStruct(like.sha...  63 us
    all_to_all x2, starting transfers between devices, exchange(): lax.all_to_all(inner, 'gy', split_axis=0, concat_axis=0, tiled=True)  47.6 us
    ppermute x6, starting transfers between devices, exchange(): lax.ppermute(block, 'gx', [(p, (p + k + 1) % count) for p in range(count)])  12 us
    pallas_call x1, Pallas kernels, pack(): pl.pallas_call(pack_kernel, out_shape=[jax.ShapeDtypeStruct((inner_count,...  3.92 us
  transfers between devices with their start and end apart: 8, of which 2 were waited for; matrix products, arithmetic and copies ran while one was open for 2% of the time, Pallas kernels for 0%

profile of v1, /device:TPU:0, one launch (start us, length us, event | category | flops | bytes accessed | tf_op | source)
XLA Modules:
  0.0 134.2 jit_solution(18386938874645423291)
XLA Ops:
  0.0 0.7 pad_add_fusion.here_ref.refs_2_
  0.7 3.9 %shard_map.55 = (f32[8,56,128]{2,1,0:T(8,128)}, f32[56,128]{1,0:T(8,128)}, f32[56,128]{1,0:T(8,128)}, f32[56,128]{1,0:T(8,128)}) custom-call(s32[2]{0:T(128)} %pad_add_fusion.here_ref.refs_2_, s32[1,1536]{1,0:T(1,128)} %index_ref.1, f32[56,1280]{1,0:T(8,128)} %refs_6_.1), custom_call_target="tpu_custom_call" | custom-call | tf_op jit(solution)/shard_map/pallas_call | solution.py:399
  4.6 5.2 %all-to-all-start = ((f32[8,56,128]{2,1,0:T(8,128)}), f32[8,56,128]{2,1,0:T(8,128)S(1)}, u32[]{:S(2)}, u32[]{:S(2)}) async-start(f32[8,56,128]{2,1,0:T(8,128)} %get-tuple-element.14), calls=%async_computation | async-start | bytes 458752 | tf_op jit(solution)/shard_map/all_to_all | solution.py:452
  9.8 1.6 %collective-permute-start = (f32[56,128]{1,0:T(8,128)}, f32[56,128]{1,0:T(8,128)S(1)}, u32[]{:S(2)}, u32[]{:S(2)}) collective-permute-start(f32[56,128]{1,0:T(8,128)} %get-tuple-element.15), channel_id=1, source_target_pairs={{0,8},{8,16},{16,24},{24,0},{1,9},{9,17},{17,25},{25,1},{2,10},{10... | collective-permute-start | bytes 86024 | tf_op jit(solution)/shard_map/ppermute | solution.py:450
  11.3 2.6 %collective-permute-start.1 = (f32[56,128]{1,0:T(8,128)}, f32[56,128]{1,0:T(8,128)S(1)}, u32[]{:S(2)}, u32[]{:S(2)}) collective-permute-start(f32[56,128]{1,0:T(8,128)} %get-tuple-element.16), channel_id=1, source_target_pairs={{0,16},{8,24},{16,0},{24,8},{1,17},{9,25},{17,1},{25,9},{2,18},{10... | collective-permute-start | bytes 86024 | tf_op jit(solution)/shard_map/ppermute | solution.py:450
  13.9 1.3 %collective-permute-start.2 = (f32[56,128]{1,0:T(8,128)}, f32[56,128]{1,0:T(8,128)S(1)}, u32[]{:S(2)}, u32[]{:S(2)}) collective-permute-start(f32[56,128]{1,0:T(8,128)} %get-tuple-element.17), channel_id=1, source_target_pairs={{0,24},{8,0},{16,8},{24,16},{1,25},{9,1},{17,9},{25,17},{2,26},{10... | collective-permute-start | bytes 86024 | tf_op jit(solution)/shard_map/ppermute | solution.py:450
  15.3 1.1 convert_reduce_fusion.1
  16.4 0.3 reduce-window.9
  16.7 0.1 slice.10
  16.9 0.1 slice_reduce_fusion
  17.0 0.1 add_bitcast_fusion
  17.0 0.4 convert_reduce_fusion
  17.5 0.1 add_multiply_fusion.refs_0_
  17.6 0.4 collective-permute-done.2.refs_11_
  18.0 0.0 all-to-all-done.refs_8_
  18.0 0.7 copy-done.1
  18.7 63.0 %shard_map.56 = (f32[56,1280]{1,0:T(8,128)S(1)}, f32[8,56,128]{2,1,0:T(8,128)}, f32[56,128]{1,0:T(8,128)S(1)}, f32[56,128]{1,0:T(8,128)S(1)}, f32[56,128]{1,0:T(8,128)S(1)}) custom-call(s32[317]{0:T(512)S(1)} %add_multiply_fusion.refs_0_, s32[2592]{0:T(1024)S(1)} %broadcast_minimum_fusion.refs_1_, s32[2]{0:T(128)S(1)} %copy-done.1, s32[316,256]{1,0:T(8,128)} %refs_3_.1, ...), custom_call_target="tpu_custom_call" | custom-call | flops 99999997952 | bytes 12000000 | tf_op jit(solution)/shard_map/pallas_call | solution.py:347
  81.7 42.4 %all-to-all-start.1 = ((f32[8,56,128]{2,1,0:T(8,128)}), f32[8,56,128]{2,1,0:T(8,128)S(1)}, u32[]{:S(2)}, u32[]{:S(2)}) async-start(f32[8,56,128]{2,1,0:T(8,128)} %get-tuple-element.19), calls=%async_computation.1 | async-start | bytes 458752 | tf_op jit(solution)/shard_map/all_to_all | solution.py:452
  124.1 3.6 %collective-permute-start.4 = (f32[56,128]{1,0:T(8,128)S(1)}, f32[56,128]{1,0:T(8,128)S(1)}, u32[]{:S(2)}, u32[]{:S(2)}) collective-permute-start(f32[56,128]{1,0:T(8,128)S(1)} %get-tuple-element.21), channel_id=1, source_target_pairs={{0,16},{8,24},{16,0},{24,8},{1,17},{9,25},{17,1},{25,9},{2,18},{10... | collective-permute-start | bytes 86024 | tf_op jit(solution)/shard_map/ppermute | solution.py:450
  127.7 2.9 %collective-permute-start.5 = (f32[56,128]{1,0:T(8,128)S(1)}, f32[56,128]{1,0:T(8,128)S(1)}, u32[]{:S(2)}, u32[]{:S(2)}) collective-permute-start(f32[56,128]{1,0:T(8,128)S(1)} %get-tuple-element.22), channel_id=1, source_target_pairs={{0,24},{8,0},{16,8},{24,16},{1,25},{9,1},{17,9},{25,17},{2,26},{10... | collective-permute-start | bytes 86024 | tf_op jit(solution)/shard_map/ppermute | solution.py:450
  130.5 0.0 collective-permute-done.3.refs_0_
  130.5 0.0 collective-permute-done.4.refs_1_
  130.6 1.6 %collective-permute-done.5.refs_2_ = f32[56,128]{1,0:T(8,128)S(1)} collective-permute-done((f32[56,128]{1,0:T(8,128)S(1)}, f32[56,128]{1,0:T(8,128)S(1)}, u32[]{:S(2)}, u32[]{:S(2)}) %collective-permute-start.5) | collective-permute-done | bytes 28704 | tf_op jit(solution)/shard_map/ppermute | solution.py:450
  132.1 2.1 %shard_map.57 = f32[56,1280]{1,0:T(8,128)} custom-call(s32[2]{0:T(128)S(1)} %copy-done.2, s32[1,1536]{1,0:T(1,128)S(1)} %copy-done, f32[56,1280]{1,0:T(8,128)S(1)} %get-tuple-element.18.base_ref, f32[8,56,128]{2,1,0:T(8,128)S(1)} %all-to-all-done.1.inner_ref, f32[56,128]{1,0:T(8,128)S(1)} %collective-permute-done.3.refs_0_, ...), custom_call_target="tpu_custom_call" | custom-call | tf_op jit(solution)/shard_map/pallas_call | solution.py:434
  (14 shorter events, 0.1 us)
Async XLA Ops:
  4.6 13.4 %all-to-all-start = ((f32[8,56,128]{2,1,0:T(8,128)}), f32[8,56,128]{2,1,0:T(8,128)S(1)}, u32[]{:S(2)}, u32[]{:S(2)}) async-start(f32[8,56,128]{2,1,0:T(8,128)} %get-tuple-element.14), calls=%async_computation | async-start | bytes 458752 | tf_op jit(solution)/shard_map/all_to_all | solution.py:452
  9.8 7.8 %collective-permute-start = (f32[56,128]{1,0:T(8,128)}, f32[56,128]{1,0:T(8,128)S(1)}, u32[]{:S(2)}, u32[]{:S(2)}) collective-permute-start(f32[56,128]{1,0:T(8,128)} %get-tuple-element.15), channel_id=1, source_target_pairs={{0,8},{8,16},{16,24},{24,0},{1,9},{9,17},{17,25},{25,1},{2,10},{10... | collective-permute-start | bytes 86024 | tf_op jit(solution)/shard_map/ppermute | solution.py:450
  11.3 6.3 %collective-permute-start.1 = (f32[56,128]{1,0:T(8,128)}, f32[56,128]{1,0:T(8,128)S(1)}, u32[]{:S(2)}, u32[]{:S(2)}) collective-permute-start(f32[56,128]{1,0:T(8,128)} %get-tuple-element.16), channel_id=1, source_target_pairs={{0,16},{8,24},{16,0},{24,8},{1,17},{9,25},{17,1},{25,9},{2,18},{10... | collective-permute-start | bytes 86024 | tf_op jit(solution)/shard_map/ppermute | solution.py:450
  13.9 4.1 %collective-permute-start.2 = (f32[56,128]{1,0:T(8,128)}, f32[56,128]{1,0:T(8,128)S(1)}, u32[]{:S(2)}, u32[]{:S(2)}) collective-permute-start(f32[56,128]{1,0:T(8,128)} %get-tuple-element.17), channel_id=1, source_target_pairs={{0,24},{8,0},{16,8},{24,16},{1,25},{9,1},{17,9},{25,17},{2,26},{10... | collective-permute-start | bytes 86024 | tf_op jit(solution)/shard_map/ppermute | solution.py:450
  18.0 0.7 copy-start.1
  18.7 113.4 %copy-start = (s32[1,1536]{1,0:T(1,128)S(1)}, s32[1,1536]{1,0:T(1,128)}, u32[]{:S(2)}) copy-start(s32[1,1536]{1,0:T(1,128)} %index_ref.1) | copy-start | bytes 18436
  18.7 113.4 %copy-start.2 = (s32[2]{0:T(128)S(1)}, s32[2]{0:T(128)}, u32[]{:S(2)}) copy-start(s32[2]{0:T(128)} %pad_add_fusion.here_ref.refs_2_) | copy-start | bytes 28
  81.7 50.4 %all-to-all-start.1 = ((f32[8,56,128]{2,1,0:T(8,128)}), f32[8,56,128]{2,1,0:T(8,128)S(1)}, u32[]{:S(2)}, u32[]{:S(2)}) async-start(f32[8,56,128]{2,1,0:T(8,128)} %get-tuple-element.19), calls=%async_computation.1 | async-start | bytes 458752 | tf_op jit(solution)/shard_map/all_to_all | solution.py:452
  124.1 6.5 %collective-permute-start.3 = (f32[56,128]{1,0:T(8,128)S(1)}, f32[56,128]{1,0:T(8,128)S(1)}, u32[]{:S(2)}, u32[]{:S(2)}) collective-permute-start(f32[56,128]{1,0:T(8,128)S(1)} %get-tuple-element.20), channel_id=1, source_target_pairs={{0,8},{8,16},{16,24},{24,0},{1,9},{9,17},{17,25},{25,1},{2,10},{10... | collective-permute-start | bytes 86024 | tf_op jit(solution)/shard_map/ppermute | solution.py:450
  124.1 6.5 %collective-permute-start.4 = (f32[56,128]{1,0:T(8,128)S(1)}, f32[56,128]{1,0:T(8,128)S(1)}, u32[]{:S(2)}, u32[]{:S(2)}) collective-permute-start(f32[56,128]{1,0:T(8,128)S(1)} %get-tuple-element.21), channel_id=1, source_target_pairs={{0,16},{8,24},{16,0},{24,8},{1,17},{9,25},{17,1},{25,9},{2,18},{10... | collective-permute-start | bytes 86024 | tf_op jit(solution)/shard_map/ppermute | solution.py:450
  127.7 4.4 %collective-permute-start.5 = (f32[56,128]{1,0:T(8,128)S(1)}, f32[56,128]{1,0:T(8,128)S(1)}, u32[]{:S(2)}, u32[]{:S(2)}) collective-permute-start(f32[56,128]{1,0:T(8,128)S(1)} %get-tuple-element.22), channel_id=1, source_target_pairs={{0,24},{8,0},{16,8},{24,16},{1,25},{9,1},{17,9},{25,17},{2,26},{10... | collective-permute-start | bytes 86024 | tf_op jit(solution)/shard_map/ppermute | solution.py:450

commit v2 on v1

--- a/solution.py
+++ b/solution.py
@@ -114,13 +114,13 @@
 def turn_matrices(t_ref, matrix_ref):
     terms, _, offset_count = t_ref.shape
     turns = batch_of(terms, 4)
-    pad = jnp.zeros((LANES - 2 * terms, offset_count), jnp.float32)
 
     def turn(step, carry):
         for u in range(turns):
             i = step * turns + u
-            block = t_ref[i]
-            matrix_ref[pl.ds(i, offset_count, stride=terms), :] = jnp.concatenate([block, block, pad], axis=0).T
+            parts = stack_parts(t_ref[i]).T.astype(jnp.float32)
+            pad = jnp.zeros((offset_count, LANES - 2 * terms), jnp.float32)
+            matrix_ref[pl.ds(i, offset_count, stride=terms), :] = jnp.concatenate([parts, pad], axis=1)
         return carry
 
     lax.fori_loop(0, terms // turns, turn, 0)
@@ -154,7 +154,7 @@
         for c, mask in enumerate(masks):
             some = jnp.where(mask, found[c * parts + r : c * parts + r + 8], some)
         picked.append(some)
-    return jnp.concatenate(picked, axis=0).astype(jnp.bfloat16)
+    return jnp.concatenate(picked, axis=0)
 
 
 def block_for(place, here, sign):
@@ -199,7 +199,7 @@
         inner_ref[place] = read(outer_count + block, there)
         return carry
 
-    lax.fori_loop(0, inner_ref.shape[0], hand, 0)
+    lax.fori_loop(0, inner_ref.shape[0], hand, 0, unroll=4)
 
 
 def take_in(put, here_ref, sign, outer_refs, inner_ref):
@@ -279,8 +279,6 @@
     steps = (starts_ref[starts_ref.shape[0] - 1] + (WIDTH - 1)) // WIDTH
     low_lanes = lax.broadcasted_iota(jnp.int32, (terms, 2 * LANES), 1) & (LANES - 1)
 
-    once = lax.broadcasted_iota(jnp.int32, (grains * terms, LANES), 1) < terms
-
     def scatter(group):
         first = jnp.maximum(group, 0) * per_step
         own_acc_ref[...] += scatter_product(index_row(target_ref, first, per_step), own_half, forward_ref[...])
@@ -295,18 +293,18 @@
             sources = gather_columns(
                 own_columns(x_ref) + [near_ref.at[k] for k in range(spare)], source_ref[pl.ds(row, 1), :]
             )
-            columns = jnp.concatenate([stack_parts(sources), targets[:, q * LANES : (q + 1) * LANES]], axis=1)
-            gap = jnp.zeros((LANES - parts, 2 * LANES), jnp.bfloat16)
-            columns = jnp.concatenate([columns, gap, columns[:SHORT]], axis=0)
-            high, low = [], []
-            for g in range(grains):
-                offset = offsets_ref[row * grains + g]
-                matrix = t_ref[pl.ds(pl.multiple_of(offset * terms, 8), terms), :]
-                high.append(matrix.astype(jnp.bfloat16).astype(jnp.float32))
-                low.append(matrix - high[-1])
-            high = jnp.concatenate(high, axis=0).astype(jnp.bfloat16)
-            low = jnp.where(once, jnp.concatenate(low, axis=0), 0.0).astype(jnp.bfloat16)
-            matrices = jnp.concatenate([high, low], axis=1)[:, : LANES + SHORT]
+            here = slice(q * LANES, (q + 1) * LANES)
+            source_high = sources.astype(jnp.bfloat16).astype(jnp.float32)
+            high = jnp.concatenate([source_high, targets[:terms, here]], axis=1)
+            low = jnp.concatenate([sources - source_high, targets[terms:, here]], axis=1)
+            gap = jnp.zeros((LANES - parts, 2 * LANES), jnp.float32)
+            rest = jnp.zeros((SHORT - terms, 2 * LANES), jnp.float32)
+            columns = jnp.concatenate([high, high, gap, low, rest], axis=0).astype(jnp.bfloat16)
+            matrices = [
+                t_ref[pl.ds(pl.multiple_of(offsets_ref[row * grains + g] * terms, 8), terms), :] for g in range(grains)
+            ]
+            matrices = jnp.concatenate(matrices, axis=0).astype(jnp.bfloat16)
+            matrices = jnp.concatenate([matrices, matrices[:, :SHORT]], axis=1)
             moved = jnp.dot(matrices, columns, preferred_element_type=jnp.float32)
             total = moved[:terms]
             for g in range(1, grains):

time: 136 us -> 133 us (0.978); the launches traced: 134 us -> 133 us
  starting transfers between devices: 59.5 us -> 55.1 us
  Pallas kernels: 69 us -> 70.6 us
    ppermute x6, starting transfers between devices: 12 us -> 9.33 us  [exchange(): lax.ppermute(block, 'gx', [(p, (p + k + 1) % count) for p in range(count)])]
    pallas_call x1, Pallas kernels: 63 us -> 65.1 us  [translate(): pl.pallas_call(translate_kernel, out_shape=[jax.ShapeDtypeStruct(like.sha...]
    all_to_all x2, starting transfers between devices: 47.6 us -> 45.8 us  [exchange(): lax.all_to_all(inner, 'gy', split_axis=0, concat_axis=0, tiled=True)]
  transfers between devices with their start and end apart: 8 -> 8, of which waited for: 2 -> 4; matrix products, arithmetic and copies ran while one was open for 2% -> 2% of each run, Pallas kernels for 0% -> 0%
where the time goes in v2:
time: 133 us
  Pallas kernels  70.6 us (53%)
  starting transfers between devices  55.1 us (41%)
  waiting for transfers between devices  3.18 us (2%)
  other arithmetic  2.74 us (2%)
    pallas_call x1, Pallas kernels, translate(): pl.pallas_call(translate_kernel, out_shape=[jax.ShapeDtypeStruct(like.sha...  65.1 us
    all_to_all x2, starting transfers between devices, exchange(): lax.all_to_all(inner, 'gy', split_axis=0, concat_axis=0, tiled=True)  45.8 us
    ppermute x6, starting transfers between devices, exchange(): lax.ppermute(block, 'gx', [(p, (p + k + 1) % count) for p in range(count)])  9.33 us
    pallas_call x1, Pallas kernels, pack(): pl.pallas_call(pack_kernel, out_shape=[jax.ShapeDtypeStruct((inner_count,...  3.43 us
    ppermute x6, waiting for transfers between devices, exchange(): lax.ppermute(block, 'gx', [(p, (p + k + 1) % count) for p in range(count)])  2.83 us
  transfers between devices with their start and end apart: 8, of which 4 were waited for; matrix products, arithmetic and copies ran while one was open for 2% of the time, Pallas kernels for 0%

profile of v2, /device:TPU:0, one launch (start us, length us, event | category | flops | bytes accessed | tf_op | source)
XLA Modules:
  0.0 132.6 jit_solution(3949628082139819376)
XLA Ops:
  0.0 0.7 pad_add_fusion.here_ref.refs_2_
  0.7 3.4 %shard_map.55 = (f32[8,56,128]{2,1,0:T(8,128)}, f32[56,128]{1,0:T(8,128)}, f32[56,128]{1,0:T(8,128)}, f32[56,128]{1,0:T(8,128)}) custom-call(s32[2]{0:T(128)} %pad_add_fusion.here_ref.refs_2_, s32[1,1536]{1,0:T(1,128)} %index_ref.1, f32[56,1280]{1,0:T(8,128)} %refs_6_.1), custom_call_target="tpu_custom_call" | custom-call | tf_op jit(solution)/shard_map/pallas_call | solution.py:397
  4.1 5.2 %all-to-all-start = ((f32[8,56,128]{2,1,0:T(8,128)}), f32[8,56,128]{2,1,0:T(8,128)S(1)}, u32[]{:S(2)}, u32[]{:S(2)}) async-start(f32[8,56,128]{2,1,0:T(8,128)} %get-tuple-element.14), calls=%async_computation | async-start | bytes 458752 | tf_op jit(solution)/shard_map/all_to_all | solution.py:450
  9.3 1.6 %collective-permute-start = (f32[56,128]{1,0:T(8,128)}, f32[56,128]{1,0:T(8,128)S(1)}, u32[]{:S(2)}, u32[]{:S(2)}) collective-permute-start(f32[56,128]{1,0:T(8,128)} %get-tuple-element.15), channel_id=1, source_target_pairs={{0,8},{8,16},{16,24},{24,0},{1,9},{9,17},{17,25},{25,1},{2,10},{10... | collective-permute-start | bytes 86024 | tf_op jit(solution)/shard_map/ppermute | solution.py:448
  10.9 2.6 %collective-permute-start.1 = (f32[56,128]{1,0:T(8,128)}, f32[56,128]{1,0:T(8,128)S(1)}, u32[]{:S(2)}, u32[]{:S(2)}) collective-permute-start(f32[56,128]{1,0:T(8,128)} %get-tuple-element.16), channel_id=1, source_target_pairs={{0,16},{8,24},{16,0},{24,8},{1,17},{9,25},{17,1},{25,9},{2,18},{10... | collective-permute-start | bytes 86024 | tf_op jit(solution)/shard_map/ppermute | solution.py:448
  13.5 1.3 %collective-permute-start.2 = (f32[56,128]{1,0:T(8,128)}, f32[56,128]{1,0:T(8,128)S(1)}, u32[]{:S(2)}, u32[]{:S(2)}) collective-permute-start(f32[56,128]{1,0:T(8,128)} %get-tuple-element.17), channel_id=1, source_target_pairs={{0,24},{8,0},{16,8},{24,16},{1,25},{9,1},{17,9},{25,17},{2,26},{10... | collective-permute-start | bytes 86024 | tf_op jit(solution)/shard_map/ppermute | solution.py:448
  14.8 1.1 convert_reduce_fusion.1
  15.9 0.3 reduce-window.9
  16.2 0.1 slice.10
  16.4 0.1 slice_reduce_fusion
  16.5 0.1 add_bitcast_fusion
  16.6 0.4 convert_reduce_fusion
  17.0 0.1 add_multiply_fusion.refs_0_
  17.1 0.0 collective-permute-done.refs_9_
  17.1 0.4 collective-permute-done.2.refs_11_
  17.5 0.7 copy-done.1
  18.2 65.1 %shard_map.56 = (f32[56,1280]{1,0:T(8,128)S(1)}, f32[8,56,128]{2,1,0:T(8,128)}, f32[56,128]{1,0:T(8,128)S(1)}, f32[56,128]{1,0:T(8,128)S(1)}, f32[56,128]{1,0:T(8,128)S(1)}) custom-call(s32[317]{0:T(512)S(1)} %add_multiply_fusion.refs_0_, s32[2592]{0:T(1024)S(1)} %broadcast_minimum_fusion.refs_1_, s32[2]{0:T(128)S(1)} %copy-done.1, s32[316,256]{1,0:T(8,128)} %refs_3_.1, ...), custom_call_target="tpu_custom_call" | custom-call | flops 99999997952 | bytes 12000000 | tf_op jit(solution)/shard_map/pallas_call | solution.py:345
  83.3 40.6 %all-to-all-start.1 = ((f32[8,56,128]{2,1,0:T(8,128)}), f32[8,56,128]{2,1,0:T(8,128)S(1)}, u32[]{:S(2)}, u32[]{:S(2)}) async-start(f32[8,56,128]{2,1,0:T(8,128)} %get-tuple-element.19), calls=%async_computation.1 | async-start | bytes 458752 | tf_op jit(solution)/shard_map/all_to_all | solution.py:450
  124.0 0.1 collective-permute-start.4
  124.1 3.7 %collective-permute-start.5 = (f32[56,128]{1,0:T(8,128)S(1)}, f32[56,128]{1,0:T(8,128)S(1)}, u32[]{:S(2)}, u32[]{:S(2)}) collective-permute-start(f32[56,128]{1,0:T(8,128)S(1)} %get-tuple-element.22), channel_id=1, source_target_pairs={{0,24},{8,0},{16,8},{24,16},{1,25},{9,1},{17,9},{25,17},{2,26},{10... | collective-permute-start | bytes 86024 | tf_op jit(solution)/shard_map/ppermute | solution.py:448
  127.8 2.1 %collective-permute-done.3.refs_0_ = f32[56,128]{1,0:T(8,128)S(1)} collective-permute-done((f32[56,128]{1,0:T(8,128)S(1)}, f32[56,128]{1,0:T(8,128)S(1)}, u32[]{:S(2)}, u32[]{:S(2)}) %collective-permute-start.3) | collective-permute-done | bytes 28704 | tf_op jit(solution)/shard_map/ppermute | solution.py:448
  129.9 0.3 collective-permute-done.5.refs_2_
  130.2 0.3 all-to-all-done.1.inner_ref
  130.6 2.1 %shard_map.57 = f32[56,1280]{1,0:T(8,128)} custom-call(s32[2]{0:T(128)S(1)} %copy-done.2, s32[1,1536]{1,0:T(1,128)S(1)} %copy-done, f32[56,1280]{1,0:T(8,128)S(1)} %get-tuple-element.18.base_ref, f32[8,56,128]{2,1,0:T(8,128)S(1)} %all-to-all-done.1.inner_ref, f32[56,128]{1,0:T(8,128)S(1)} %collective-permute-done.3.refs_0_, ...), custom_call_target="tpu_custom_call" | custom-call | tf_op jit(solution)/shard_map/pallas_call | solution.py:432
  (14 shorter events, 0.1 us)
Async XLA Ops:
  4.1 13.4 %all-to-all-start = ((f32[8,56,128]{2,1,0:T(8,128)}), f32[8,56,128]{2,1,0:T(8,128)S(1)}, u32[]{:S(2)}, u32[]{:S(2)}) async-start(f32[8,56,128]{2,1,0:T(8,128)} %get-tuple-element.14), calls=%async_computation | async-start | bytes 458752 | tf_op jit(solution)/shard_map/all_to_all | solution.py:450
  9.3 7.8 %collective-permute-start = (f32[56,128]{1,0:T(8,128)}, f32[56,128]{1,0:T(8,128)S(1)}, u32[]{:S(2)}, u32[]{:S(2)}) collective-permute-start(f32[56,128]{1,0:T(8,128)} %get-tuple-element.15), channel_id=1, source_target_pairs={{0,8},{8,16},{16,24},{24,0},{1,9},{9,17},{17,25},{25,1},{2,10},{10... | collective-permute-start | bytes 86024 | tf_op jit(solution)/shard_map/ppermute | solution.py:448
  10.9 6.3 %collective-permute-start.1 = (f32[56,128]{1,0:T(8,128)}, f32[56,128]{1,0:T(8,128)S(1)}, u32[]{:S(2)}, u32[]{:S(2)}) collective-permute-start(f32[56,128]{1,0:T(8,128)} %get-tuple-element.16), channel_id=1, source_target_pairs={{0,16},{8,24},{16,0},{24,8},{1,17},{9,25},{17,1},{25,9},{2,18},{10... | collective-permute-start | bytes 86024 | tf_op jit(solution)/shard_map/ppermute | solution.py:448
  13.5 4.1 %collective-permute-start.2 = (f32[56,128]{1,0:T(8,128)}, f32[56,128]{1,0:T(8,128)S(1)}, u32[]{:S(2)}, u32[]{:S(2)}) collective-permute-start(f32[56,128]{1,0:T(8,128)} %get-tuple-element.17), channel_id=1, source_target_pairs={{0,24},{8,0},{16,8},{24,16},{1,25},{9,1},{17,9},{25,17},{2,26},{10... | collective-permute-start | bytes 86024 | tf_op jit(solution)/shard_map/ppermute | solution.py:448
  17.5 0.7 copy-start.1
  18.2 112.3 %copy-start = (s32[1,1536]{1,0:T(1,128)S(1)}, s32[1,1536]{1,0:T(1,128)}, u32[]{:S(2)}) copy-start(s32[1,1536]{1,0:T(1,128)} %index_ref.1) | copy-start | bytes 18436
  18.2 112.3 %copy-start.2 = (s32[2]{0:T(128)S(1)}, s32[2]{0:T(128)}, u32[]{:S(2)}) copy-start(s32[2]{0:T(128)} %pad_add_fusion.here_ref.refs_2_) | copy-start | bytes 28
  83.3 47.2 %all-to-all-start.1 = ((f32[8,56,128]{2,1,0:T(8,128)}), f32[8,56,128]{2,1,0:T(8,128)S(1)}, u32[]{:S(2)}, u32[]{:S(2)}) async-start(f32[8,56,128]{2,1,0:T(8,128)} %get-tuple-element.19), calls=%async_computation.1 | async-start | bytes 458752 | tf_op jit(solution)/shard_map/all_to_all | solution.py:450
  124.0 5.9 %collective-permute-start.3 = (f32[56,128]{1,0:T(8,128)S(1)}, f32[56,128]{1,0:T(8,128)S(1)}, u32[]{:S(2)}, u32[]{:S(2)}) collective-permute-start(f32[56,128]{1,0:T(8,128)S(1)} %get-tuple-element.20), channel_id=1, source_target_pairs={{0,8},{8,16},{16,24},{24,0},{1,9},{9,17},{17,25},{25,1},{2,10},{10... | collective-permute-start | bytes 86024 | tf_op jit(solution)/shard_map/ppermute | solution.py:448
  124.0 5.9 %collective-permute-start.4 = (f32[56,128]{1,0:T(8,128)S(1)}, f32[56,128]{1,0:T(8,128)S(1)}, u32[]{:S(2)}, u32[]{:S(2)}) collective-permute-start(f32[56,128]{1,0:T(8,128)S(1)} %get-tuple-element.21), channel_id=1, source_target_pairs={{0,16},{8,24},{16,0},{24,8},{1,17},{9,25},{17,1},{25,9},{2,18},{10... | collective-permute-start | bytes 86024 | tf_op jit(solution)/shard_map/ppermute | solution.py:448
  124.1 6.1 %collective-permute-start.5 = (f32[56,128]{1,0:T(8,128)S(1)}, f32[56,128]{1,0:T(8,128)S(1)}, u32[]{:S(2)}, u32[]{:S(2)}) collective-permute-start(f32[56,128]{1,0:T(8,128)S(1)} %get-tuple-element.22), channel_id=1, source_target_pairs={{0,24},{8,0},{16,8},{24,16},{1,25},{9,1},{17,9},{25,17},{2,26},{10... | collective-permute-start | bytes 86024 | tf_op jit(solution)/shard_map/ppermute | solution.py:448

commit v3 on v2

--- a/solution.py
+++ b/solution.py
@@ -11,7 +11,8 @@
 LANES = 128
 SUBLANES = 16
 WIDTH = 1024
-GRAIN = 32
+GRAIN = 64
+TOGETHER = 2
 FOLD = 256
 SCRATCHES = 14
 SHORT = 64
@@ -130,16 +131,18 @@
     return jnp.concatenate([ref[pl.ds(first + q, 1), :] for q in range(count)], axis=1)
 
 
-def gather_columns(parts, index):
+def gather_columns(parts, rows):
     terms = parts[0].shape[0]
-    lane = jnp.broadcast_to(index & (LANES - 1), (terms, LANES))
-    chunk = jnp.broadcast_to(index >> 7, (8, LANES))
-    picked = [jnp.zeros((8, LANES), jnp.float32)] * (terms // 8)
+    lanes = [jnp.broadcast_to(index & (LANES - 1), (terms, LANES)) for index in rows]
+    chunks = [jnp.broadcast_to(index >> 7, (8, LANES)) for index in rows]
+    picked = [[jnp.zeros((8, LANES), jnp.float32)] * (terms // 8) for _ in rows]
     for c, part in enumerate(parts):
-        found = jnp.take_along_axis(part[...], lane, axis=1, mode="promise_in_bounds")
-        here = chunk == c
-        picked = [jnp.where(here, found[8 * r : 8 * r + 8], some) for r, some in enumerate(picked)]
-    return jnp.concatenate(picked, axis=0)
+        cells = part[...]
+        for k, lane in enumerate(lanes):
+            found = jnp.take_along_axis(cells, lane, axis=1, mode="promise_in_bounds")
+            here = chunks[k] == c
+            picked[k] = [jnp.where(here, found[8 * r : 8 * r + 8], some) for r, some in enumerate(picked[k])]
+    return [jnp.concatenate(some, axis=0) for some in picked]
 
 
 def fold_columns(fold_ref, parts, index):
@@ -290,9 +293,12 @@
         targets = fold_columns(fold_ref, parts, index_row(target_ref, group * per_step, per_step))
         for q in range(per_step):
             row = group * per_step + q
-            sources = gather_columns(
-                own_columns(x_ref) + [near_ref.at[k] for k in range(spare)], source_ref[pl.ds(row, 1), :]
-            )
+            if q % TOGETHER == 0:
+                gathered = gather_columns(
+                    own_columns(x_ref) + [near_ref.at[k] for k in range(spare)],
+                    [source_ref[pl.ds(row + k, 1), :] for k in range(TOGETHER)],
+                )
+            sources = gathered[q % TOGETHER]
             here = slice(q * LANES, (q + 1) * LANES)
             source_high = sources.astype(jnp.bfloat16).astype(jnp.float32)
             high = jnp.concatenate([source_high, targets[:terms, here]], axis=1)
@@ -384,7 +390,7 @@
     def read(block, there):
         index = index_ref[:, pl.ds(pl.multiple_of(block * LANES, LANES), LANES)]
         index = index if there is True else jnp.where(there, index, -1)
-        return gather_columns([x_ref.at[:, c * LANES : (c + 1) * LANES] for c in range(cells // LANES)], index)
+        return gather_columns([x_ref.at[:, c * LANES : (c + 1) * LANES] for c in range(cells // LANES)], [index])[0]
 
     hand_out(read, here_ref, -1, outer_refs, inner_ref)
 

time: 133 us -> 147 us (1.11); the launches traced: 133 us -> 145 us
  Pallas kernels: 70.6 us -> 101 us
  starting transfers between devices: 55.1 us -> 36.6 us
    pallas_call x1, Pallas kernels: 65.1 us -> 95.8 us  [translate(): pl.pallas_call(translate_kernel, out_shape=[jax.ShapeDtypeStruct(like.sha...]
    all_to_all x2, starting transfers between devices: 45.8 us -> 27.3 us  [exchange(): lax.all_to_all(inner, 'gy', split_axis=0, concat_axis=0, tiled=True)]
  transfers between devices with their start and end apart: 8 -> 8, of which waited for: 4 -> 4; matrix products, arithmetic and copies ran while one was open for 2% -> 1% of each run, Pallas kernels for 0% -> 0%
where the time goes in v3:
time: 147 us; the launch traced here: 145 us
  Pallas kernels  101 us (69%)
  starting transfers between devices  36.6 us (25%)
  waiting for transfers between devices  3.35 us (2%)
  other arithmetic  2.58 us (2%)
    pallas_call x1, Pallas kernels, translate(): pl.pallas_call(translate_kernel, out_shape=[jax.ShapeDtypeStruct(like.sha...  95.8 us
    all_to_all x2, starting transfers between devices, exchange(): lax.all_to_all(inner, 'gy', split_axis=0, concat_axis=0, tiled=True)  27.3 us
    ppermute x6, starting transfers between devices, exchange(): lax.ppermute(block, 'gx', [(p, (p + k + 1) % count) for p in range(count)])  9.33 us
    pallas_call x1, Pallas kernels, pack(): pl.pallas_call(pack_kernel, out_shape=[jax.ShapeDtypeStruct((inner_count,...  3.43 us
    ppermute x6, waiting for transfers between devices, exchange(): lax.ppermute(block, 'gx', [(p, (p + k + 1) % count) for p in range(count)])  3 us
  transfers between devices with their start and end apart: 8, of which 4 were waited for; matrix products, arithmetic and copies ran while one was open for 1% of the time, Pallas kernels for 0%

profile of v3, /device:TPU:0, one launch (start us, length us, event | category | flops | bytes accessed | tf_op | source)
XLA Modules:
  0.0 144.8 jit_solution(12755993676397719494)
XLA Ops:
  0.0 0.7 pad_add_fusion.here_ref.refs_2_
  0.7 3.4 %shard_map.55 = (f32[8,56,128]{2,1,0:T(8,128)}, f32[56,128]{1,0:T(8,128)}, f32[56,128]{1,0:T(8,128)}, f32[56,128]{1,0:T(8,128)}) custom-call(s32[2]{0:T(128)} %pad_add_fusion.here_ref.refs_2_, s32[1,1536]{1,0:T(1,128)} %index_ref.1, f32[56,1280]{1,0:T(8,128)} %refs_6_.1), custom_call_target="tpu_custom_call" | custom-call | tf_op jit(solution)/shard_map/pallas_call | solution.py:403
  4.1 5.2 %all-to-all-start = ((f32[8,56,128]{2,1,0:T(8,128)}), f32[8,56,128]{2,1,0:T(8,128)S(1)}, u32[]{:S(2)}, u32[]{:S(2)}) async-start(f32[8,56,128]{2,1,0:T(8,128)} %get-tuple-element.14), calls=%async_computation | async-start | bytes 458752 | tf_op jit(solution)/shard_map/all_to_all | solution.py:456
  9.3 1.6 %collective-permute-start = (f32[56,128]{1,0:T(8,128)}, f32[56,128]{1,0:T(8,128)S(1)}, u32[]{:S(2)}, u32[]{:S(2)}) collective-permute-start(f32[56,128]{1,0:T(8,128)} %get-tuple-element.15), channel_id=1, source_target_pairs={{0,8},{8,16},{16,24},{24,0},{1,9},{9,17},{17,25},{25,1},{2,10},{10... | collective-permute-start | bytes 86024 | tf_op jit(solution)/shard_map/ppermute | solution.py:454
  10.9 2.6 %collective-permute-start.1 = (f32[56,128]{1,0:T(8,128)}, f32[56,128]{1,0:T(8,128)S(1)}, u32[]{:S(2)}, u32[]{:S(2)}) collective-permute-start(f32[56,128]{1,0:T(8,128)} %get-tuple-element.16), channel_id=1, source_target_pairs={{0,16},{8,24},{16,0},{24,8},{1,17},{9,25},{17,1},{25,9},{2,18},{10... | collective-permute-start | bytes 86024 | tf_op jit(solution)/shard_map/ppermute | solution.py:454
  13.5 1.3 collective-permute-start.2
  14.8 1.1 convert_reduce_fusion.1
  15.9 0.3 reduce-window.9
  16.2 0.1 slice.10
  16.4 0.1 slice_reduce_fusion
  16.5 0.1 add_bitcast_fusion
  16.6 0.3 convert_reduce_fusion
  16.9 0.1 add_multiply_fusion.refs_0_
  16.9 0.0 collective-permute-done.1.refs_10_
  16.9 0.6 collective-permute-done.2.refs_11_
  17.5 0.7 copy-done.1
  18.2 95.8 %shard_map.56 = (f32[56,1280]{1,0:T(8,128)S(1)}, f32[8,56,128]{2,1,0:T(8,128)}, f32[56,128]{1,0:T(8,128)S(1)}, f32[56,128]{1,0:T(8,128)S(1)}, f32[56,128]{1,0:T(8,128)S(1)}) custom-call(s32[317]{0:T(512)S(1)} %add_multiply_fusion.refs_0_, s32[1296]{0:T(1024)S(1)} %broadcast_minimum_fusion.refs_1_, s32[2]{0:T(128)S(1)} %copy-done.1, s32[316,256]{1,0:T(8,128)} %refs_3_.1, ...), custom_call_target="tpu_custom_call" | custom-call | flops 99999997952 | bytes 12000000 | tf_op jit(solution)/shard_map/pallas_call | solution.py:351
  114.1 22.1 %all-to-all-start.1 = ((f32[8,56,128]{2,1,0:T(8,128)}), f32[8,56,128]{2,1,0:T(8,128)S(1)}, u32[]{:S(2)}, u32[]{:S(2)}) async-start(f32[8,56,128]{2,1,0:T(8,128)} %get-tuple-element.19), calls=%async_computation.1 | async-start | bytes 458752 | tf_op jit(solution)/shard_map/all_to_all | solution.py:456
  136.2 0.4 collective-permute-start.4
  136.6 3.4 %collective-permute-start.5 = (f32[56,128]{1,0:T(8,128)S(1)}, f32[56,128]{1,0:T(8,128)S(1)}, u32[]{:S(2)}, u32[]{:S(2)}) collective-permute-start(f32[56,128]{1,0:T(8,128)S(1)} %get-tuple-element.22), channel_id=1, source_target_pairs={{0,24},{8,0},{16,8},{24,16},{1,25},{9,1},{17,9},{25,17},{2,26},{10... | collective-permute-start | bytes 86024 | tf_op jit(solution)/shard_map/ppermute | solution.py:454
  140.0 2.1 %collective-permute-done.3.refs_0_ = f32[56,128]{1,0:T(8,128)S(1)} collective-permute-done((f32[56,128]{1,0:T(8,128)S(1)}, f32[56,128]{1,0:T(8,128)S(1)}, u32[]{:S(2)}, u32[]{:S(2)}) %collective-permute-start.3) | collective-permute-done | bytes 28704 | tf_op jit(solution)/shard_map/ppermute | solution.py:454
  142.1 0.3 collective-permute-done.5.refs_2_
  142.4 0.3 all-to-all-done.1.inner_ref
  142.8 2.1 %shard_map.57 = f32[56,1280]{1,0:T(8,128)} custom-call(s32[2]{0:T(128)S(1)} %copy-done.2, s32[1,1536]{1,0:T(1,128)S(1)} %copy-done, f32[56,1280]{1,0:T(8,128)S(1)} %get-tuple-element.18.base_ref, f32[8,56,128]{2,1,0:T(8,128)S(1)} %all-to-all-done.1.inner_ref, f32[56,128]{1,0:T(8,128)S(1)} %collective-permute-done.3.refs_0_, ...), custom_call_target="tpu_custom_call" | custom-call | tf_op jit(solution)/shard_map/pallas_call | solution.py:438
  (14 shorter events, 0.1 us)
Async XLA Ops:
  4.1 13.4 %all-to-all-start = ((f32[8,56,128]{2,1,0:T(8,128)}), f32[8,56,128]{2,1,0:T(8,128)S(1)}, u32[]{:S(2)}, u32[]{:S(2)}) async-start(f32[8,56,128]{2,1,0:T(8,128)} %get-tuple-element.14), calls=%async_computation | async-start | bytes 458752 | tf_op jit(solution)/shard_map/all_to_all | solution.py:456
  9.3 7.7 %collective-permute-start = (f32[56,128]{1,0:T(8,128)}, f32[56,128]{1,0:T(8,128)S(1)}, u32[]{:S(2)}, u32[]{:S(2)}) collective-permute-start(f32[56,128]{1,0:T(8,128)} %get-tuple-element.15), channel_id=1, source_target_pairs={{0,8},{8,16},{16,24},{24,0},{1,9},{9,17},{17,25},{25,1},{2,10},{10... | collective-permute-start | bytes 86024 | tf_op jit(solution)/shard_map/ppermute | solution.py:454
  10.9 6.1 %collective-permute-start.1 = (f32[56,128]{1,0:T(8,128)}, f32[56,128]{1,0:T(8,128)S(1)}, u32[]{:S(2)}, u32[]{:S(2)}) collective-permute-start(f32[56,128]{1,0:T(8,128)} %get-tuple-element.16), channel_id=1, source_target_pairs={{0,16},{8,24},{16,0},{24,8},{1,17},{9,25},{17,1},{25,9},{2,18},{10... | collective-permute-start | bytes 86024 | tf_op jit(solution)/shard_map/ppermute | solution.py:454
  13.5 4.1 %collective-permute-start.2 = (f32[56,128]{1,0:T(8,128)}, f32[56,128]{1,0:T(8,128)S(1)}, u32[]{:S(2)}, u32[]{:S(2)}) collective-permute-start(f32[56,128]{1,0:T(8,128)} %get-tuple-element.17), channel_id=1, source_target_pairs={{0,24},{8,0},{16,8},{24,16},{1,25},{9,1},{17,9},{25,17},{2,26},{10... | collective-permute-start | bytes 86024 | tf_op jit(solution)/shard_map/ppermute | solution.py:454
  17.5 0.7 copy-start.1
  18.2 124.5 %copy-start = (s32[1,1536]{1,0:T(1,128)S(1)}, s32[1,1536]{1,0:T(1,128)}, u32[]{:S(2)}) copy-start(s32[1,1536]{1,0:T(1,128)} %index_ref.1) | copy-start | bytes 18436
  18.2 124.5 %copy-start.2 = (s32[2]{0:T(128)S(1)}, s32[2]{0:T(128)}, u32[]{:S(2)}) copy-start(s32[2]{0:T(128)} %pad_add_fusion.here_ref.refs_2_) | copy-start | bytes 28
  114.1 28.7 %all-to-all-start.1 = ((f32[8,56,128]{2,1,0:T(8,128)}), f32[8,56,128]{2,1,0:T(8,128)S(1)}, u32[]{:S(2)}, u32[]{:S(2)}) async-start(f32[8,56,128]{2,1,0:T(8,128)} %get-tuple-element.19), calls=%async_computation.1 | async-start | bytes 458752 | tf_op jit(solution)/shard_map/all_to_all | solution.py:456
  136.2 5.9 %collective-permute-start.3 = (f32[56,128]{1,0:T(8,128)S(1)}, f32[56,128]{1,0:T(8,128)S(1)}, u32[]{:S(2)}, u32[]{:S(2)}) collective-permute-start(f32[56,128]{1,0:T(8,128)S(1)} %get-tuple-element.20), channel_id=1, source_target_pairs={{0,8},{8,16},{16,24},{24,0},{1,9},{9,17},{17,25},{25,1},{2,10},{10... | collective-permute-start | bytes 86024 | tf_op jit(solution)/shard_map/ppermute | solution.py:454
  136.2 5.9 %collective-permute-start.4 = (f32[56,128]{1,0:T(8,128)S(1)}, f32[56,128]{1,0:T(8,128)S(1)}, u32[]{:S(2)}, u32[]{:S(2)}) collective-permute-start(f32[56,128]{1,0:T(8,128)S(1)} %get-tuple-element.21), channel_id=1, source_target_pairs={{0,16},{8,24},{16,0},{24,8},{1,17},{9,25},{17,1},{25,9},{2,18},{10... | collective-permute-start | bytes 86024 | tf_op jit(solution)/shard_map/ppermute | solution.py:454
  136.6 5.8 %collective-permute-start.5 = (f32[56,128]{1,0:T(8,128)S(1)}, f32[56,128]{1,0:T(8,128)S(1)}, u32[]{:S(2)}, u32[]{:S(2)}) collective-permute-start(f32[56,128]{1,0:T(8,128)S(1)} %get-tuple-element.22), channel_id=1, source_target_pairs={{0,24},{8,0},{16,8},{24,16},{1,25},{9,1},{17,9},{25,17},{2,26},{10... | collective-permute-start | bytes 86024 | tf_op jit(solution)/shard_map/ppermute | solution.py:454

commit v4 on v2

--- a/solution.py
+++ b/solution.py
@@ -12,8 +12,9 @@
 SUBLANES = 16
 WIDTH = 1024
 GRAIN = 32
+DIRECT = 2
 FOLD = 256
-SCRATCHES = 14
+SCRATCHES = 15
 SHORT = 64
 PACK_LIMIT = 60 * 1024 * 1024
 VMEM_LIMIT = 53 * 1024 * 1024
@@ -224,7 +225,7 @@
     starts_ref, offsets_ref, here_ref, pair_target_ref, pair_source_ref, trans_ref, multipoles_ref, sign_ref, inner_ref,
     outer_refs, own_ref, inner_back_ref, outer_back_refs,
     target_pairs_ref, source_pairs_ref, native_ref, x_ref, target_ref, source_ref, t_ref,
-    fold_ref, near_ref, forward_ref, backward_ref, own_acc_ref, all_acc_ref, ready
+    fold_ref, signed_ref, near_ref, forward_ref, backward_ref, own_acc_ref, all_acc_ref, ready
 ):
     fetches = [
         pltpu.make_async_copy(here, there, ready.at[k])
@@ -252,8 +253,9 @@
     for fetch in fetches[:3]:
         fetch.wait()
     folds = cells // FOLD
+    signed_ref[...] = x_ref[...] * sign_ref[...]
     for c in range(folds):
-        fold_ref[c * parts : (c + 1) * parts, :] = stack_parts(x_ref[:, c * FOLD : (c + 1) * FOLD] * sign_ref[...])
+        fold_ref[c * parts : (c + 1) * parts, :] = stack_parts(signed_ref[:, c * FOLD : (c + 1) * FOLD])
     near_ref[...] = jnp.zeros_like(near_ref)
 
     def put(block, there, value):
@@ -287,16 +289,22 @@
     def step(group, carry):
         scatter(group - 1)
         ahead, back = [], []
-        targets = fold_columns(fold_ref, parts, index_row(target_ref, group * per_step, per_step))
+        targets = fold_columns(fold_ref, parts, index_row(target_ref, group * per_step + DIRECT, per_step - DIRECT))
         for q in range(per_step):
             row = group * per_step + q
             sources = gather_columns(
                 own_columns(x_ref) + [near_ref.at[k] for k in range(spare)], source_ref[pl.ds(row, 1), :]
             )
-            here = slice(q * LANES, (q + 1) * LANES)
-            source_high = sources.astype(jnp.bfloat16).astype(jnp.float32)
-            high = jnp.concatenate([source_high, targets[:terms, here]], axis=1)
-            low = jnp.concatenate([sources - source_high, targets[terms:, here]], axis=1)
+            if q < DIRECT:
+                direct = gather_columns(own_columns(signed_ref), target_ref[pl.ds(row, 1), :])
+                both = jnp.concatenate([sources, direct], axis=1)
+                high = both.astype(jnp.bfloat16).astype(jnp.float32)
+                low = both - high
+            else:
+                here = slice((q - DIRECT) * LANES, (q - DIRECT + 1) * LANES)
+                source_high = sources.astype(jnp.bfloat16).astype(jnp.float32)
+                high = jnp.concatenate([source_high, targets[:terms, here]], axis=1)
+                low = jnp.concatenate([sources - source_high, targets[terms:, here]], axis=1)
             gap = jnp.zeros((LANES - parts, 2 * LANES), jnp.float32)
             rest = jnp.zeros((SHORT - terms, 2 * LANES), jnp.float32)
             columns = jnp.concatenate([high, high, gap, low, rest], axis=0).astype(jnp.bfloat16)
@@ -356,6 +364,7 @@
             pltpu.VMEM((row_count, LANES), jnp.int32),
             pltpu.VMEM((offset_count * terms, LANES), jnp.float32),
             pltpu.VMEM((2 * terms * (cells // FOLD), FOLD), jnp.bfloat16),
+            pltpu.VMEM((terms, cells), jnp.float32),
             pltpu.VMEM((near_count + 1, terms, LANES), jnp.float32),
             pltpu.VMEM((2 * terms, WIDTH), jnp.bfloat16),
             pltpu.VMEM((2 * terms, WIDTH), jnp.bfloat16),

time: 133 us -> 131 us (0.985)
  Pallas kernels: 70.6 us -> 50.2 us
  starting transfers between devices: 55.1 us -> 72.5 us
    pallas_call x1, Pallas kernels: 65.1 us -> 44.7 us  [translate(): pl.pallas_call(translate_kernel, out_shape=[jax.ShapeDtypeStruct(like.sha...]
    all_to_all x2, starting transfers between devices: 45.8 us -> 63.2 us  [exchange(): lax.all_to_all(inner, 'gy', split_axis=0, concat_axis=0, tiled=True)]
where the time goes in v4:
time: 131 us; the launch traced here: 130 us
  starting transfers between devices  72.5 us (55%)
  Pallas kernels  50.2 us (38%)
  waiting for transfers between devices  3.18 us (2%)
  other arithmetic  2.74 us (2%)
    all_to_all x2, starting transfers between devices, exchange(): lax.all_to_all(inner, 'gy', split_axis=0, concat_axis=0, tiled=True)  63.2 us
    pallas_call x1, Pallas kernels, translate(): pl.pallas_call(translate_kernel, out_shape=[jax.ShapeDtypeStruct(like.sha...  44.7 us
    ppermute x6, starting transfers between devices, exchange(): lax.ppermute(block, 'gx', [(p, (p + k + 1) % count) for p in range(count)])  9.33 us
    pallas_call x1, Pallas kernels, pack(): pl.pallas_call(pack_kernel, out_shape=[jax.ShapeDtypeStruct((inner_count,...  3.43 us
    ppermute x6, waiting for transfers between devices, exchange(): lax.ppermute(block, 'gx', [(p, (p + k + 1) % count) for p in range(count)])  2.83 us
  transfers between devices with their start and end apart: 8, of which 4 were waited for; matrix products, arithmetic and copies ran while one was open for 2% of the time, Pallas kernels for 0%

profile of v4, /device:TPU:0, one launch (start us, length us, event | category | flops | bytes accessed | tf_op | source)
XLA Modules:
  0.0 129.6 jit_solution(8506013838542851492)
XLA Ops:
  0.0 0.7 pad_add_fusion.here_ref.refs_2_
  0.7 3.4 %shard_map.55 = (f32[8,56,128]{2,1,0:T(8,128)}, f32[56,128]{1,0:T(8,128)}, f32[56,128]{1,0:T(8,128)}, f32[56,128]{1,0:T(8,128)}) custom-call(s32[2]{0:T(128)} %pad_add_fusion.here_ref.refs_2_, s32[1,1536]{1,0:T(1,128)} %index_ref.1, f32[56,1280]{1,0:T(8,128)} %refs_6_.1), custom_call_target="tpu_custom_call" | custom-call | tf_op jit(solution)/shard_map/pallas_call | solution.py:406
  4.1 5.2 %all-to-all-start = ((f32[8,56,128]{2,1,0:T(8,128)}), f32[8,56,128]{2,1,0:T(8,128)S(1)}, u32[]{:S(2)}, u32[]{:S(2)}) async-start(f32[8,56,128]{2,1,0:T(8,128)} %get-tuple-element.14), calls=%async_computation | async-start | bytes 458752 | tf_op jit(solution)/shard_map/all_to_all | solution.py:459
  9.3 1.6 %collective-permute-start = (f32[56,128]{1,0:T(8,128)}, f32[56,128]{1,0:T(8,128)S(1)}, u32[]{:S(2)}, u32[]{:S(2)}) collective-permute-start(f32[56,128]{1,0:T(8,128)} %get-tuple-element.15), channel_id=1, source_target_pairs={{0,8},{8,16},{16,24},{24,0},{1,9},{9,17},{17,25},{25,1},{2,10},{10... | collective-permute-start | bytes 86024 | tf_op jit(solution)/shard_map/ppermute | solution.py:457
  10.9 2.6 %collective-permute-start.1 = (f32[56,128]{1,0:T(8,128)}, f32[56,128]{1,0:T(8,128)S(1)}, u32[]{:S(2)}, u32[]{:S(2)}) collective-permute-start(f32[56,128]{1,0:T(8,128)} %get-tuple-element.16), channel_id=1, source_target_pairs={{0,16},{8,24},{16,0},{24,8},{1,17},{9,25},{17,1},{25,9},{2,18},{10... | collective-permute-start | bytes 86024 | tf_op jit(solution)/shard_map/ppermute | solution.py:457
  13.5 1.3 %collective-permute-start.2 = (f32[56,128]{1,0:T(8,128)}, f32[56,128]{1,0:T(8,128)S(1)}, u32[]{:S(2)}, u32[]{:S(2)}) collective-permute-start(f32[56,128]{1,0:T(8,128)} %get-tuple-element.17), channel_id=1, source_target_pairs={{0,24},{8,0},{16,8},{24,16},{1,25},{9,1},{17,9},{25,17},{2,26},{10... | collective-permute-start | bytes 86024 | tf_op jit(solution)/shard_map/ppermute | solution.py:457
  14.8 1.1 convert_reduce_fusion.1
  15.9 0.3 reduce-window.9
  16.2 0.1 slice.10
  16.4 0.1 slice_reduce_fusion
  16.5 0.1 add_bitcast_fusion
  16.6 0.4 convert_reduce_fusion
  17.0 0.1 add_multiply_fusion.refs_0_
  17.1 0.0 collective-permute-done.refs_9_
  17.1 0.4 collective-permute-done.2.refs_11_
  17.5 0.7 copy-done.1
  18.2 44.7 %shard_map.56 = (f32[56,1280]{1,0:T(8,128)S(1)}, f32[8,56,128]{2,1,0:T(8,128)}, f32[56,128]{1,0:T(8,128)S(1)}, f32[56,128]{1,0:T(8,128)S(1)}, f32[56,128]{1,0:T(8,128)S(1)}) custom-call(s32[317]{0:T(512)S(1)} %add_multiply_fusion.refs_0_, s32[2592]{0:T(1024)S(1)} %broadcast_minimum_fusion.refs_1_, s32[2]{0:T(128)S(1)} %copy-done.1, s32[316,256]{1,0:T(8,128)} %refs_3_.1, ...), custom_call_target="tpu_custom_call" | custom-call | flops 99999997952 | bytes 12000000 | tf_op jit(solution)/shard_map/pallas_call | solution.py:353
  62.9 58.0 %all-to-all-start.1 = ((f32[8,56,128]{2,1,0:T(8,128)}), f32[8,56,128]{2,1,0:T(8,128)S(1)}, u32[]{:S(2)}, u32[]{:S(2)}) async-start(f32[8,56,128]{2,1,0:T(8,128)} %get-tuple-element.19), calls=%async_computation.1 | async-start | bytes 458752 | tf_op jit(solution)/shard_map/all_to_all | solution.py:459
  121.0 0.9 collective-permute-start.4
  121.9 2.9 %collective-permute-start.5 = (f32[56,128]{1,0:T(8,128)S(1)}, f32[56,128]{1,0:T(8,128)S(1)}, u32[]{:S(2)}, u32[]{:S(2)}) collective-permute-start(f32[56,128]{1,0:T(8,128)S(1)} %get-tuple-element.22), channel_id=1, source_target_pairs={{0,24},{8,0},{16,8},{24,16},{1,25},{9,1},{17,9},{25,17},{2,26},{10... | collective-permute-start | bytes 86024 | tf_op jit(solution)/shard_map/ppermute | solution.py:457
  124.8 2.1 %collective-permute-done.3.refs_0_ = f32[56,128]{1,0:T(8,128)S(1)} collective-permute-done((f32[56,128]{1,0:T(8,128)S(1)}, f32[56,128]{1,0:T(8,128)S(1)}, u32[]{:S(2)}, u32[]{:S(2)}) %collective-permute-start.3) | collective-permute-done | bytes 28704 | tf_op jit(solution)/shard_map/ppermute | solution.py:457
  126.9 0.3 collective-permute-done.5.refs_2_
  127.2 0.3 all-to-all-done.1.inner_ref
  127.6 2.1 %shard_map.57 = f32[56,1280]{1,0:T(8,128)} custom-call(s32[2]{0:T(128)S(1)} %copy-done.2, s32[1,1536]{1,0:T(1,128)S(1)} %copy-done, f32[56,1280]{1,0:T(8,128)S(1)} %get-tuple-element.18.base_ref, f32[8,56,128]{2,1,0:T(8,128)S(1)} %all-to-all-done.1.inner_ref, f32[56,128]{1,0:T(8,128)S(1)} %collective-permute-done.3.refs_0_, ...), custom_call_target="tpu_custom_call" | custom-call | tf_op jit(solution)/shard_map/pallas_call | solution.py:441
  (14 shorter events, 0.1 us)
Async XLA Ops:
  4.1 13.4 %all-to-all-start = ((f32[8,56,128]{2,1,0:T(8,128)}), f32[8,56,128]{2,1,0:T(8,128)S(1)}, u32[]{:S(2)}, u32[]{:S(2)}) async-start(f32[8,56,128]{2,1,0:T(8,128)} %get-tuple-element.14), calls=%async_computation | async-start | bytes 458752 | tf_op jit(solution)/shard_map/all_to_all | solution.py:459
  9.3 7.8 %collective-permute-start = (f32[56,128]{1,0:T(8,128)}, f32[56,128]{1,0:T(8,128)S(1)}, u32[]{:S(2)}, u32[]{:S(2)}) collective-permute-start(f32[56,128]{1,0:T(8,128)} %get-tuple-element.15), channel_id=1, source_target_pairs={{0,8},{8,16},{16,24},{24,0},{1,9},{9,17},{17,25},{25,1},{2,10},{10... | collective-permute-start | bytes 86024 | tf_op jit(solution)/shard_map/ppermute | solution.py:457
  10.9 6.3 %collective-permute-start.1 = (f32[56,128]{1,0:T(8,128)}, f32[56,128]{1,0:T(8,128)S(1)}, u32[]{:S(2)}, u32[]{:S(2)}) collective-permute-start(f32[56,128]{1,0:T(8,128)} %get-tuple-element.16), channel_id=1, source_target_pairs={{0,16},{8,24},{16,0},{24,8},{1,17},{9,25},{17,1},{25,9},{2,18},{10... | collective-permute-start | bytes 86024 | tf_op jit(solution)/shard_map/ppermute | solution.py:457
  13.5 4.1 %collective-permute-start.2 = (f32[56,128]{1,0:T(8,128)}, f32[56,128]{1,0:T(8,128)S(1)}, u32[]{:S(2)}, u32[]{:S(2)}) collective-permute-start(f32[56,128]{1,0:T(8,128)} %get-tuple-element.17), channel_id=1, source_target_pairs={{0,24},{8,0},{16,8},{24,16},{1,25},{9,1},{17,9},{25,17},{2,26},{10... | collective-permute-start | bytes 86024 | tf_op jit(solution)/shard_map/ppermute | solution.py:457
  17.5 0.7 copy-start.1
  18.2 109.3 %copy-start = (s32[1,1536]{1,0:T(1,128)S(1)}, s32[1,1536]{1,0:T(1,128)}, u32[]{:S(2)}) copy-start(s32[1,1536]{1,0:T(1,128)} %index_ref.1) | copy-start | bytes 18436
  18.2 109.3 %copy-start.2 = (s32[2]{0:T(128)S(1)}, s32[2]{0:T(128)}, u32[]{:S(2)}) copy-start(s32[2]{0:T(128)} %pad_add_fusion.here_ref.refs_2_) | copy-start | bytes 28
  62.9 64.6 %all-to-all-start.1 = ((f32[8,56,128]{2,1,0:T(8,128)}), f32[8,56,128]{2,1,0:T(8,128)S(1)}, u32[]{:S(2)}, u32[]{:S(2)}) async-start(f32[8,56,128]{2,1,0:T(8,128)} %get-tuple-element.19), calls=%async_computation.1 | async-start | bytes 458752 | tf_op jit(solution)/shard_map/all_to_all | solution.py:459
  121.0 5.9 %collective-permute-start.3 = (f32[56,128]{1,0:T(8,128)S(1)}, f32[56,128]{1,0:T(8,128)S(1)}, u32[]{:S(2)}, u32[]{:S(2)}) collective-permute-start(f32[56,128]{1,0:T(8,128)S(1)} %get-tuple-element.20), channel_id=1, source_target_pairs={{0,8},{8,16},{16,24},{24,0},{1,9},{9,17},{17,25},{25,1},{2,10},{10... | collective-permute-start | bytes 86024 | tf_op jit(solution)/shard_map/ppermute | solution.py:457
  121.0 5.9 %collective-permute-start.4 = (f32[56,128]{1,0:T(8,128)S(1)}, f32[56,128]{1,0:T(8,128)S(1)}, u32[]{:S(2)}, u32[]{:S(2)}) collective-permute-start(f32[56,128]{1,0:T(8,128)S(1)} %get-tuple-element.21), channel_id=1, source_target_pairs={{0,16},{8,24},{16,0},{24,8},{1,17},{9,25},{17,1},{25,9},{2,18},{10... | collective-permute-start | bytes 86024 | tf_op jit(solution)/shard_map/ppermute | solution.py:457
  121.9 5.3 %collective-permute-start.5 = (f32[56,128]{1,0:T(8,128)S(1)}, f32[56,128]{1,0:T(8,128)S(1)}, u32[]{:S(2)}, u32[]{:S(2)}) collective-permute-start(f32[56,128]{1,0:T(8,128)S(1)} %get-tuple-element.22), channel_id=1, source_target_pairs={{0,24},{8,0},{16,8},{24,16},{1,25},{9,1},{17,9},{25,17},{2,26},{10... | collective-permute-start | bytes 86024 | tf_op jit(solution)/shard_map/ppermute | solution.py:457
